TPU v7x, 512 devices: a whole 4x4x16 slice. The times are simulated.
512 devices in a mesh: section: 4 (over y), dp: 32 (over x, z_lo), tensor: 4 (over z_hi, core).
Axes of the slice: x: 4, y: 4, z: 16 (z_hi: 2, z_lo: 8; z = z_hi * 8 + z_lo), core: 2. Of those that a mesh axis runs over, the one named last changes fastest.
Arguments:
- stored_copies: bfloat16 [4, 2, 4096, 9216], P('section', None, 'dp', 'tensor'), may hold values from -80 to 80, as said below
- entry_codes: bfloat16 [4096, 9216], P('dp', 'tensor'), may hold values from -1 to 1
- exit_grad_codes: bfloat16 [4096, 9216], P('dp', 'tensor'), may hold values from -1 to 1
- exit_grad_scales: float32 [4096], P('dp'), may hold values from 0 to 0.28125, as said below
- slot_ids: int32 [32, 4], P('dp'), may hold values from 0 to 3, each once within a row
- norm_gain: float32 [4, 9216], P('section', 'tensor'), may hold values from 0.1 to 1.9
- down_proj: bfloat16 [4, 384, 9216], P('section', 'dp', 'tensor'), may hold values from -0.0625 to 0.0625
- up_proj: bfloat16 [4, 384, 9216], P('section', 'dp', 'tensor'), may hold values from -0.3125 to 0.3125
Outputs:
- sent_codes: bfloat16 [4, 4096, 9216], P('section', 'dp', 'tensor')
- returned_codes: bfloat16 [4, 4096, 9216], P('section', 'dp', 'tensor')
- grad_down: float32 [4, 384, 9216], P('section', 'dp', 'tensor')
- grad_up: float32 [4, 384, 9216], P('section', 'dp', 'tensor')
Inputs may be any that keep to these rules, and one draw needn't show every extreme that they name: `stored_copies`: the output copy of each section but the last equals the input copy of the next section. `exit_grad_scales`: Positive. `slot_ids`: each row holds every slot number once.
All inputs are finite; a program needn't handle non-finite values. Where the computation divides by a largest or mean magnitude, that divisor is 1e-20 or more.
Results may differ from a plain program's by a relative error of at most 0.033.
Values may be sent and summed in bfloat16 or wider, within the bound.
A program may use at most 64 MiB of HBM per device.

v0:
```python
import jax
import jax.numpy as jnp
from jax import lax
from jax.sharding import PartitionSpec as P

D = 9216
MICRO = 4
ROWS = 32


def from_behind(block, axis, distance):
    devices = range(lax.axis_size(axis))
    route = [(i - distance, i) for i in devices if i - distance in devices]
    return lax.ppermute(block, axis, route)


def contract_rows(left_side, right_side):
    return lax.dot_general(
        left_side, right_side, (((0,), (0,)), ((), ())), preferred_element_type=jnp.float32
    )


def contract_cols(left_side, right_side):
    return lax.dot_general(
        left_side, right_side, (((1,), (1,)), ((), ())), preferred_element_type=jnp.float32
    )


def gelu_slope(inner_rows, grad_out):
    unused_value, pull_back = jax.vjp(jax.nn.gelu, inner_rows)
    return pull_back(grad_out)[0]


def put_rows(buffer, new_rows, row_start, is_live):
    old_rows = lax.dynamic_slice_in_dim(buffer, row_start, new_rows.shape[0], 0)
    return lax.dynamic_update_slice_in_dim(
        buffer, jnp.where(is_live, new_rows, old_rows), row_start, 0
    )


def take_rows(source, row_start):
    return lax.dynamic_slice_in_dim(source, row_start, ROWS, 0)


def norm_rows(section_input):
    row_mean = lax.psum(jnp.sum(section_input, 1), "tensor") / D
    centred = section_input - row_mean[:, None]
    variance = lax.psum(jnp.sum(centred * centred, 1), "tensor") / D
    inverse_scale = lax.rsqrt(variance + 1e-05)
    return ((section_input - row_mean[:, None]) * inverse_scale[:, None], inverse_scale)


def local(
    stored_copies,
    entry_codes,
    exit_grad_codes,
    exit_grad_scales,
    slot_ids,
    norm_gain,
    down_proj,
    up_proj,
):
    section_index = lax.axis_index("section")
    sections = lax.axis_size("section")
    tick_count = MICRO + sections - 1
    copies = stored_copies[0].astype(jnp.float32)
    squares = lax.psum(jnp.sum(copies * copies, 2), "tensor")
    copy_spans = 2.0 * jnp.sqrt(squares / D + 1e-05)
    slot_order = slot_ids[0]
    gain_row = norm_gain[0]
    down_full, up_full = (
        lax.all_gather(down_proj[0], "dp", axis=0, tiled=True),
        lax.all_gather(up_proj[0], "dp", axis=0, tiled=True),
    )
    row_total = entry_codes.shape[0]
    local_features = entry_codes.shape[1]
    bottleneck = down_full.shape[0]

    def forward_tick(carry, tick_index):
        incoming, normed_store, scale_store, scaled_store, inner_store, hidden_store, sent_store = (
            carry
        )
        micro_index = tick_index - section_index
        is_live = (micro_index >= 0) & (micro_index < MICRO)
        micro_safe = jnp.clip(micro_index, 0, MICRO - 1)
        row_start = micro_safe * ROWS
        copy_start = slot_order[micro_safe] * ROWS
        copy_in = take_rows(copies[0], copy_start)
        span_in = take_rows(copy_spans[0], copy_start)
        arrived = jnp.where(section_index == 0, take_rows(entry_codes, row_start), incoming)
        section_input = copy_in + span_in[:, None] * arrived.astype(jnp.float32)
        normed, inverse_scale = norm_rows(section_input)
        scaled = (normed * gain_row).astype(jnp.bfloat16)
        inner_rows = lax.psum(contract_cols(scaled, down_full), "tensor")
        hidden = jax.nn.gelu(inner_rows).astype(jnp.bfloat16)
        result = section_input + jnp.dot(hidden, up_full, preferred_element_type=jnp.float32)
        copy_out = take_rows(copies[1], copy_start)
        span_out = take_rows(copy_spans[1], copy_start)
        codes_out = jnp.clip((result - copy_out) / span_out[:, None], -1.0, 1.0).astype(
            jnp.bfloat16
        )
        passed = from_behind(codes_out, "section", 1)
        new_carry = (
            passed,
            put_rows(normed_store, normed, row_start, is_live),
            put_rows(scale_store, inverse_scale, row_start, is_live),
            put_rows(scaled_store, scaled, row_start, is_live),
            put_rows(inner_store, inner_rows, row_start, is_live),
            put_rows(hidden_store, hidden, row_start, is_live),
            put_rows(sent_store, codes_out, row_start, is_live),
        )
        return (new_carry, None)

    start_forward = (
        jnp.zeros((ROWS, local_features), jnp.bfloat16),
        jnp.zeros((row_total, local_features), jnp.float32),
        jnp.zeros((row_total,), jnp.float32),
        jnp.zeros((row_total, local_features), jnp.bfloat16),
        jnp.zeros((row_total, bottleneck), jnp.float32),
        jnp.zeros((row_total, bottleneck), jnp.bfloat16),
        jnp.zeros((row_total, local_features), jnp.bfloat16),
    )
    forward_state, unused_out = lax.scan(forward_tick, start_forward, jnp.arange(tick_count))
    unused_codes, normed_store, scale_store, scaled_store, inner_store, hidden_store, sent_store = (
        forward_state
    )

    def backward_tick(carry, tick_index):
        incoming, incoming_peak, grad_parts, code_store = carry
        micro_index = tick_index - (sections - 1 - section_index)
        is_live = (micro_index >= 0) & (micro_index < MICRO)
        micro_safe = jnp.clip(micro_index, 0, MICRO - 1)
        row_start = micro_safe * ROWS
        exit_rows = take_rows(exit_grad_codes, row_start).astype(jnp.float32)
        exit_scale = take_rows(exit_grad_scales, row_start)
        from_exit = exit_rows * exit_scale[:, None]
        from_next = incoming.astype(jnp.float32) * incoming_peak.astype(jnp.float32)[:, None]
        upstream = jnp.where(section_index == sections - 1, from_exit, from_next)
        upstream_half = upstream.astype(jnp.bfloat16)
        normed = take_rows(normed_store, row_start)
        inverse_scale = take_rows(scale_store, row_start)
        scaled = take_rows(scaled_store, row_start)
        inner_rows = take_rows(inner_store, row_start)
        hidden = take_rows(hidden_store, row_start)
        back_grad = lax.psum(contract_cols(upstream_half, up_full), "tensor")
        grad_inner = gelu_slope(inner_rows, back_grad).astype(jnp.bfloat16)
        grad_parts = (
            grad_parts[0] + jnp.where(is_live, contract_rows(grad_inner, scaled), 0.0),
            grad_parts[1] + jnp.where(is_live, contract_rows(hidden, upstream_half), 0.0),
        )
        grad_normed = jnp.dot(grad_inner, down_full, preferred_element_type=jnp.float32) * gain_row
        sum_grad, sum_cross = lax.psum(
            (jnp.sum(grad_normed, 1), jnp.sum(grad_normed * normed, 1)), "tensor"
        )
        grad_input = upstream + inverse_scale[:, None] * (
            grad_normed - sum_grad[:, None] / D - normed * (sum_cross[:, None] / D)
        )
        row_peak = (lax.pmax(jnp.max(jnp.abs(grad_input), 1), "tensor") + 1e-05).astype(
            jnp.bfloat16
        )
        codes_back = (grad_input / row_peak.astype(jnp.float32)[:, None]).astype(jnp.bfloat16)
        passed, passed_peak = from_behind((codes_back, row_peak), "section", -1)
        code_store = put_rows(code_store, codes_back, row_start, is_live)
        return ((passed, passed_peak, grad_parts, code_store), None)

    start_parts = (
        jnp.zeros((bottleneck, local_features), jnp.float32),
        jnp.zeros((bottleneck, local_features), jnp.float32),
    )
    start_backward = (
        jnp.zeros((ROWS, local_features), jnp.bfloat16),
        jnp.zeros((ROWS,), jnp.bfloat16),
        start_parts,
        jnp.zeros((row_total, local_features), jnp.bfloat16),
    )
    backward_state, unused_back = lax.scan(backward_tick, start_backward, jnp.arange(tick_count))
    unused_grad, unused_peak, grad_parts, code_store = backward_state
    grad_down, grad_up = (
        lax.psum_scatter(
            grad_parts[0].astype(jnp.bfloat16), "dp", scatter_dimension=0, tiled=True
        ).astype(jnp.float32),
        lax.psum_scatter(
            grad_parts[1].astype(jnp.bfloat16), "dp", scatter_dimension=0, tiled=True
        ).astype(jnp.float32),
    )
    return (sent_store[None], code_store[None], grad_down[None], grad_up[None])


def solution(mesh):
    in_specs = (
        P("section", None, "dp", "tensor"),
        P("dp", "tensor"),
        P("dp", "tensor"),
        P("dp"),
        P("dp", None),
        P("section", "tensor"),
        P("section", "dp", "tensor"),
        P("section", "dp", "tensor"),
    )
    out_specs = (
        P("section", "dp", "tensor"),
        P("section", "dp", "tensor"),
        P("section", "dp", "tensor"),
        P("section", "dp", "tensor"),
    )
    return jax.shard_map(local, mesh=mesh, in_specs=in_specs, out_specs=out_specs, check_vma=False)
```

profile of v0, /device:TPU:6, one launch (start us, length us, event | category | flops | bytes accessed | tf_op | source)
XLA Modules:
  0.0 1928.0 jit_solution(15612554703659015968)
XLA Ops:
  12.3 27.9 %psum.61 = f32[2,128]{1,0:T(2,128)S(1)} all-reduce(f32[2,128]{1,0:T(2,128)S(1)} %multiply_reduce_fusion.2), channel_id=1, replica_groups=mesh['section'=4,'dp'=32,'tensor'=4] {'tensor'}, use_global_device_ids=true, to_apply=%region_1.0 | all-reduce | flops 256 | bytes 2048 | tf_op jit(solution)/shard_map/psum | solution.py:67
  41.7 189.5 %all-gather.5.cloned.1.call-done = bf16[1,384,2304]{2,0,1:T(2,128)(2,1)} async-done(((bf16[1,12,2304]{2,0,1:T(2,128)(2,1)}), bf16[1,384,2304]{2,0,1:T(2,128)(2,1)}) %all-gather.5.cloned.1.call-update) | async-done | bytes 1769488 | tf_op jit(solution)/shard_map/all_gather | solution.py:72
  234.7 232.0 %all-gather.7.cloned.1.call-done = bf16[1,384,2304]{2,0,1:T(2,128)(2,1)} async-done(((bf16[1,12,2304]{2,0,1:T(2,128)(2,1)}), bf16[1,384,2304]{2,0,1:T(2,128)(2,1)}) %all-gather.7.cloned.1.call-update) | async-done | bytes 1769488 | tf_op jit(solution)/shard_map/all_gather | solution.py:73
  473.1 594.5 %while.44 = (s32[]{:T(128)}, bf16[32,2304]{1,0:T(8,128)(2,1)S(1)}, f32[128,2304]{1,0:T(8,128)}, f32[128]{0:T(128)S(1)}, bf16[128,2304]{1,0:T(8,128)(2,1)}, /*ind...) while((s32[]{:T(128)}, bf16[32,2304]{1,0:T(8,128)(2,1)S(1)}, ...), condition=%wide.region_8.9_spmd, body=%wide.region_2.8_spmd.sunk | while | flops 115421328 | bytes 13314417 | solution.py:123
  479.9 15.8 psum.69
  495.9 25.0 %psum.70 = f32[32]{0:T(128)S(1)} all-reduce(f32[32]{0:T(128)S(1)} %multiply_reduce_fusion.4), channel_id=1, replica_groups=mesh['section'=4,'dp'=32,'tensor'=4] {'tensor'}, use_global_device_ids=true, to_apply=%region_6.6 | all-reduce | flops 32 | bytes 256 | tf_op jit(solution)/shard_map/while/body/eval_jaxpr/psum | solution.py:48
  523.9 28.1 %psum.71 = f32[32,384]{1,0:T(8,128)S(1)} all-reduce(f32[32,384]{1,0:T(8,128)S(1)} %fusion.79), channel_id=1, replica_groups=mesh['section'=4,'dp'=32,'tensor'=4] {'tensor'}, use_global_device_ids=true, to_apply=%region_7.7 | all-reduce | flops 12288 | bytes 98304 | tf_op jit(solution)/shard_map/while/body/eval_jaxpr/psum | solution.py:94
  602.9 36.5 %psum.71 = f32[32,384]{1,0:T(8,128)S(1)} all-reduce(f32[32,384]{1,0:T(8,128)S(1)} %fusion.79), channel_id=1, replica_groups=mesh['section'=4,'dp'=32,'tensor'=4] {'tensor'}, use_global_device_ids=true, to_apply=%region_7.7 | all-reduce | flops 12288 | bytes 98304 | tf_op jit(solution)/shard_map/while/body/eval_jaxpr/psum | solution.py:94
  691.3 28.0 %psum.71 = f32[32,384]{1,0:T(8,128)S(1)} all-reduce(f32[32,384]{1,0:T(8,128)S(1)} %fusion.79), channel_id=1, replica_groups=mesh['section'=4,'dp'=32,'tensor'=4] {'tensor'}, use_global_device_ids=true, to_apply=%region_7.7 | all-reduce | flops 12288 | bytes 98304 | tf_op jit(solution)/shard_map/while/body/eval_jaxpr/psum | solution.py:94
  737.2 21.9 %psum.69 = f32[32]{0:T(128)S(1)} all-reduce(f32[32]{0:T(128)S(1)} %get-tuple-element.810), channel_id=1, replica_groups=mesh['section'=4,'dp'=32,'tensor'=4] {'tensor'}, use_global_device_ids=true, to_apply=%region_4.4 | all-reduce | flops 32 | bytes 256 | tf_op jit(solution)/shard_map/while/body/eval_jaxpr/psum | solution.py:46
  777.8 28.5 %psum.71 = f32[32,384]{1,0:T(8,128)S(1)} all-reduce(f32[32,384]{1,0:T(8,128)S(1)} %fusion.79), channel_id=1, replica_groups=mesh['section'=4,'dp'=32,'tensor'=4] {'tensor'}, use_global_device_ids=true, to_apply=%region_7.7 | all-reduce | flops 12288 | bytes 98304 | tf_op jit(solution)/shard_map/while/body/eval_jaxpr/psum | solution.py:94
  838.2 22.4 %psum.70 = f32[32]{0:T(128)S(1)} all-reduce(f32[32]{0:T(128)S(1)} %multiply_reduce_fusion.4), channel_id=1, replica_groups=mesh['section'=4,'dp'=32,'tensor'=4] {'tensor'}, use_global_device_ids=true, to_apply=%region_6.6 | all-reduce | flops 32 | bytes 256 | tf_op jit(solution)/shard_map/while/body/eval_jaxpr/psum | solution.py:48
  863.6 28.7 %psum.71 = f32[32,384]{1,0:T(8,128)S(1)} all-reduce(f32[32,384]{1,0:T(8,128)S(1)} %fusion.79), channel_id=1, replica_groups=mesh['section'=4,'dp'=32,'tensor'=4] {'tensor'}, use_global_device_ids=true, to_apply=%region_7.7 | all-reduce | flops 12288 | bytes 98304 | tf_op jit(solution)/shard_map/while/body/eval_jaxpr/psum | solution.py:94
  942.5 35.3 %psum.71 = f32[32,384]{1,0:T(8,128)S(1)} all-reduce(f32[32,384]{1,0:T(8,128)S(1)} %fusion.79), channel_id=1, replica_groups=mesh['section'=4,'dp'=32,'tensor'=4] {'tensor'}, use_global_device_ids=true, to_apply=%region_7.7 | all-reduce | flops 12288 | bytes 98304 | tf_op jit(solution)/shard_map/while/body/eval_jaxpr/psum | solution.py:94
  1010.4 15.9 psum.70
  1029.3 28.1 %psum.71 = f32[32,384]{1,0:T(8,128)S(1)} all-reduce(f32[32,384]{1,0:T(8,128)S(1)} %fusion.79), channel_id=1, replica_groups=mesh['section'=4,'dp'=32,'tensor'=4] {'tensor'}, use_global_device_ids=true, to_apply=%region_7.7 | all-reduce | flops 12288 | bytes 98304 | tf_op jit(solution)/shard_map/while/body/eval_jaxpr/psum | solution.py:94
  1069.1 625.0 %while.45 = (s32[]{:T(128)}, bf16[32,2304]{1,0:T(8,128)(2,1)}, bf16[32]{0:T(256)(128)(2,1)S(1)}, f32[384,2304]{1,0:T(8,128)}, f32[384,2304]{1,0:T(8,128)}, /*ind...) while((s32[]{:T(128)}, bf16[32,2304]{1,0:T(8,128)(2,1)}, ...), condition=%wide.region_17.18_spmd.clone, body=%wide.region_9.17_spmd.clone.sunk | while | flops 234590416 | bytes 30102604 | solution.py:176
  1072.8 35.8 %psum.72 = f32[32,384]{1,0:T(8,128)} all-reduce(f32[32,384]{1,0:T(8,128)} %fusion.88), channel_id=1, replica_groups=mesh['section'=4,'dp'=32,'tensor'=4] {'tensor'}, use_global_device_ids=true, to_apply=%region_10.10 | all-reduce | flops 12288 | bytes 98304 | tf_op jit(solution)/shard_map/while/body/eval_jaxpr/psum | solution.py:145
  1112.8 15.8 all-reduce.7
  1160.8 29.7 %psum.72 = f32[32,384]{1,0:T(8,128)} all-reduce(f32[32,384]{1,0:T(8,128)} %fusion.88), channel_id=1, replica_groups=mesh['section'=4,'dp'=32,'tensor'=4] {'tensor'}, use_global_device_ids=true, to_apply=%region_10.10 | all-reduce | flops 12288 | bytes 98304 | tf_op jit(solution)/shard_map/while/body/eval_jaxpr/psum | solution.py:145
  1194.7 21.1 %all-reduce.7 = (f32[32]{0:T(128)S(1)}, f32[32]{0:T(128)S(1)}) all-reduce(f32[32]{0:T(128)} %get-tuple-element.834, f32[32]{0:T(128)} %get-tuple-element.835), channel_id=1, replica_groups=mesh['section'=4,'dp'=32,'tensor'=4] {'tensor'}, use_global_device_ids=true, to_apply=%region_14.14 | all-reduce | flops 64 | bytes 512 | tf_op jit(solution)/shard_map/while/body/eval_jaxpr/psum | solution.py:152
  1217.3 15.8 pmax.12
  1250.9 29.8 %psum.72 = f32[32,384]{1,0:T(8,128)} all-reduce(f32[32,384]{1,0:T(8,128)} %fusion.88), channel_id=1, replica_groups=mesh['section'=4,'dp'=32,'tensor'=4] {'tensor'}, use_global_device_ids=true, to_apply=%region_10.10 | all-reduce | flops 12288 | bytes 98304 | tf_op jit(solution)/shard_map/while/body/eval_jaxpr/psum | solution.py:145
  1301.6 21.1 %pmax.12 = f32[32]{0:T(128)S(1)} all-reduce(f32[32]{0:T(128)S(1)} %get-tuple-element.842), channel_id=1, replica_groups=mesh['section'=4,'dp'=32,'tensor'=4] {'tensor'}, use_global_device_ids=true, to_apply=%region_16.16 | all-reduce | flops 32 | bytes 256 | tf_op jit(solution)/shard_map/while/body/eval_jaxpr/pmax | solution.py:158
  1340.5 30.3 %psum.72 = f32[32,384]{1,0:T(8,128)} all-reduce(f32[32,384]{1,0:T(8,128)} %fusion.88), channel_id=1, replica_groups=mesh['section'=4,'dp'=32,'tensor'=4] {'tensor'}, use_global_device_ids=true, to_apply=%region_10.10 | all-reduce | flops 12288 | bytes 98304 | tf_op jit(solution)/shard_map/while/body/eval_jaxpr/psum | solution.py:145
  1424.9 36.1 %psum.72 = f32[32,384]{1,0:T(8,128)} all-reduce(f32[32,384]{1,0:T(8,128)} %fusion.88), channel_id=1, replica_groups=mesh['section'=4,'dp'=32,'tensor'=4] {'tensor'}, use_global_device_ids=true, to_apply=%region_10.10 | all-reduce | flops 12288 | bytes 98304 | tf_op jit(solution)/shard_map/while/body/eval_jaxpr/psum | solution.py:145
  1515.4 29.4 %psum.72 = f32[32,384]{1,0:T(8,128)} all-reduce(f32[32,384]{1,0:T(8,128)} %fusion.88), channel_id=1, replica_groups=mesh['section'=4,'dp'=32,'tensor'=4] {'tensor'}, use_global_device_ids=true, to_apply=%region_10.10 | all-reduce | flops 12288 | bytes 98304 | tf_op jit(solution)/shard_map/while/body/eval_jaxpr/psum | solution.py:145
  1549.0 21.6 %all-reduce.7 = (f32[32]{0:T(128)S(1)}, f32[32]{0:T(128)S(1)}) all-reduce(f32[32]{0:T(128)} %get-tuple-element.834, f32[32]{0:T(128)} %get-tuple-element.835), channel_id=1, replica_groups=mesh['section'=4,'dp'=32,'tensor'=4] {'tensor'}, use_global_device_ids=true, to_apply=%region_14.14 | all-reduce | flops 64 | bytes 512 | tf_op jit(solution)/shard_map/while/body/eval_jaxpr/psum | solution.py:152
  1606.3 30.1 %psum.72 = f32[32,384]{1,0:T(8,128)} all-reduce(f32[32,384]{1,0:T(8,128)} %fusion.88), channel_id=1, replica_groups=mesh['section'=4,'dp'=32,'tensor'=4] {'tensor'}, use_global_device_ids=true, to_apply=%region_10.10 | all-reduce | flops 12288 | bytes 98304 | tf_op jit(solution)/shard_map/while/body/eval_jaxpr/psum | solution.py:145
  1657.5 20.1 %pmax.12 = f32[32]{0:T(128)S(1)} all-reduce(f32[32]{0:T(128)S(1)} %get-tuple-element.842), channel_id=1, replica_groups=mesh['section'=4,'dp'=32,'tensor'=4] {'tensor'}, use_global_device_ids=true, to_apply=%region_16.16 | all-reduce | flops 32 | bytes 256 | tf_op jit(solution)/shard_map/while/body/eval_jaxpr/pmax | solution.py:158
  1697.3 136.6 %fusion.40 = (bf16[16,2304]{1,0:T(8,128)(2,1)}, bf16[16,2304]{1,0:T(8,128)(2,1)}) fusion(bf16[384,2304]{1,0:T(8,128)(2,1)S(1)} %convert_element_type.80, bf16[384,2304]{1,0:T(8,128)(2,1)S(1)} %convert_element_type.81), kind=kCustom, calls=%all-reduce-scatter.2 | all-reduce-scatter fusion | flops 2359297 | bytes 3688448
  1836.1 24.1 %collective-permute-start.9 = (bf16[16,2304]{1,0:T(8,128)(2,1)}, bf16[16,2304]{1,0:T(8,128)(2,1)S(1)}, u32[]{:S(2)}, u32[]{:S(2)}) collective-permute-start(bf16[16,2304]{1,0:T(8,128)(2,1)} %get-tuple-element.556), channel_id=1, source_target_pairs={{0,28},{4,32},{8,36},{12,40},{16,44},{20,48},{24,52},{28,56},{32,6... | collective-permute-start | bytes 221192
  (493 shorter events, 637.0 us)
Async XLA Ops:
  7.2 224.1 %all-gather.5.cloned.1.call-start = ((), (), s32[]{:S(2)}) async-start(), calls=%async_computation | async-start | bytes 3649536 | tf_op jit(solution)/shard_map/all_gather | solution.py:72
  8.9 457.8 %all-gather.7.cloned.1.call-start = ((), (), s32[]{:S(2)}) async-start(), calls=%async_computation.1 | async-start | bytes 3649536 | tf_op jit(solution)/shard_map/all_gather | solution.py:73
  554.0 10.0 collective-permute-start
  641.4 9.5 collective-permute-start
  1234.8 11.8 collective-permute-start.1
  1236.1 11.2 collective-permute-start.2
  1324.4 11.8 collective-permute-start.1
  1325.7 11.2 collective-permute-start.2
  1408.8 11.8 collective-permute-start.1
  1410.0 11.2 collective-permute-start.2
  1498.8 12.2 collective-permute-start.1
  1500.1 11.6 collective-permute-start.2
  1589.0 13.0 collective-permute-start.1
  1590.3 12.4 collective-permute-start.2
  1679.3 14.1 collective-permute-start.1
  1680.6 13.5 collective-permute-start.2
  1834.8 31.1 %collective-permute-start.10 = (bf16[12,2304]{1,0:T(8,128)(2,1)S(1)}, bf16[12,2304]{1,0:T(8,128)(2,1)S(1)}, u32[]{:S(2)}, u32[]{:S(2)}) collective-permute-start(bf16[12,2304]{1,0:T(8,128)(2,1)S(1)} %slice.16), channel_id=1, source_target_pairs={{0,32},{4,36},{8,40},{12,44},{16,48},{20,52},{24,56},{28,60},{32,6... | collective-permute-start | bytes 165896
  1836.1 31.8 %collective-permute-start.9 = (bf16[16,2304]{1,0:T(8,128)(2,1)}, bf16[16,2304]{1,0:T(8,128)(2,1)S(1)}, u32[]{:S(2)}, u32[]{:S(2)}) collective-permute-start(bf16[16,2304]{1,0:T(8,128)(2,1)} %get-tuple-element.556), channel_id=1, source_target_pairs={{0,28},{4,32},{8,36},{12,40},{16,44},{20,48},{24,52},{28,56},{32,6... | collective-permute-start | bytes 221192
  1860.2 9.7 collective-permute-start.8
  1862.1 9.8 collective-permute-start.7
  1864.0 23.5 %collective-permute-start.6 = (bf16[16,2304]{1,0:T(8,128)(2,1)}, bf16[16,2304]{1,0:T(8,128)(2,1)S(1)}, u32[]{:S(2)}, u32[]{:S(2)}) collective-permute-start(bf16[16,2304]{1,0:T(8,128)(2,1)} %get-tuple-element.556), channel_id=1, source_target_pairs={{0,16},{4,20},{8,24},{12,28},{16,32},{20,36},{24,40},{28,44},{32,4... | collective-permute-start | bytes 221192
  1866.0 25.5 %collective-permute-start.5 = (bf16[16,2304]{1,0:T(8,128)(2,1)}, bf16[16,2304]{1,0:T(8,128)(2,1)S(1)}, u32[]{:S(2)}, u32[]{:S(2)}) collective-permute-start(bf16[16,2304]{1,0:T(8,128)(2,1)} %get-tuple-element.556), channel_id=1, source_target_pairs={{0,12},{4,16},{8,20},{12,24},{16,28},{20,32},{24,36},{28,40},{32,4... | collective-permute-start | bytes 221192
  1867.9 26.8 %collective-permute-start.4 = (bf16[16,2304]{1,0:T(8,128)(2,1)}, bf16[16,2304]{1,0:T(8,128)(2,1)S(1)}, u32[]{:S(2)}, u32[]{:S(2)}) collective-permute-start(bf16[16,2304]{1,0:T(8,128)(2,1)} %get-tuple-element.556), channel_id=1, source_target_pairs={{0,8},{4,12},{8,16},{12,20},{16,24},{20,28},{24,32},{28,36},{32,40... | collective-permute-start | bytes 221192
  1869.9 26.8 %collective-permute-start.3 = (bf16[16,2304]{1,0:T(8,128)(2,1)}, bf16[16,2304]{1,0:T(8,128)(2,1)S(1)}, u32[]{:S(2)}, u32[]{:S(2)}) collective-permute-start(bf16[16,2304]{1,0:T(8,128)(2,1)} %get-tuple-element.556), channel_id=1, source_target_pairs={{0,4},{4,8},{8,12},{12,16},{16,20},{20,24},{24,28},{28,32},{32,36}... | collective-permute-start | bytes 221192
  1871.9 31.1 %collective-permute-start.17 = (bf16[16,2304]{1,0:T(8,128)(2,1)}, bf16[16,2304]{1,0:T(8,128)(2,1)S(1)}, u32[]{:S(2)}, u32[]{:S(2)}) collective-permute-start(bf16[16,2304]{1,0:T(8,128)(2,1)} %get-tuple-element.557), channel_id=1, source_target_pairs={{0,28},{4,32},{8,36},{12,40},{16,44},{20,48},{24,52},{28,56},{32,6... | collective-permute-start | bytes 221192
  1887.6 17.3 collective-permute-start.16
  1891.5 9.5 collective-permute-start.18
  1894.8 12.9 collective-permute-start.15
  1896.7 11.4 collective-permute-start.14
  1901.0 12.5 collective-permute-start.13
  1903.0 13.2 collective-permute-start.12
  1904.9 14.0 collective-permute-start.11
  (82 other events, 2245.1 us)
Sparse Core Ops, SparseCore 0:
  10.7 220.5 all-gather.4
  233.9 232.7 all-gather.6
where the time goes:
time: 1950 us; the launch traced here: 1930 us
  blocking collectives  1070 us (55%)
  waiting for transfers between devices  437 us (22%)
  matrix products  126 us (6%)
  starting transfers between devices  103 us (5%)
  other arithmetic  93.4 us (5%)
  local copies, waits for them, and re-layouts  67.2 us (3%)
    all_gather x1, waiting for transfers between devices, local(): lax.all_gather(up_proj[0], 'dp', axis=0, tiled=True)  232 us
    psum x7, blocking collectives, backward_tick(): back_grad = lax.psum(contract_cols(upstream_half, up_full), 'tensor')  221 us
    psum x7, blocking collectives, forward_tick(): inner_rows = lax.psum(contract_cols(scaled, down_full), 'tensor')  213 us
    all_gather x1, waiting for transfers between devices, local(): lax.all_gather(down_proj[0], 'dp', axis=0, tiled=True)  190 us
    unnamed x1, blocking collectives  137 us
    psum x7, blocking collectives, norm_rows(): variance = lax.psum(jnp.sum(centred * centred, 1), 'tensor') / D  124 us
    psum x7, blocking collectives, backward_tick(): lax.psum((jnp.sum(grad_normed, 1), jnp.sum(grad_normed * normed, 1)), 'te...  120 us
    pmax x7, blocking collectives, backward_tick(): lax.pmax(jnp.max(jnp.abs(grad_input), 1), 'tensor') + 1e-05  118 us
  transfers between devices with their start and end apart: 39, of which 10 were waited for; matrix products, arithmetic and copies ran while one was open for 6% of the time, Pallas kernels for 0%

commit v1 on v0

v1 whole, which is shorter than its diff:
```python
import math

import jax
import jax.numpy as jnp
from jax import lax
from jax.experimental import pallas as pl
from jax.experimental.pallas import tpu as pltpu
from jax.sharding import PartitionSpec as P

MESH = pl.DeviceIdType.MESH
F32 = jnp.float32
BF16 = jnp.bfloat16
MICRO = 4
ROWS = 32
NX = 4
PAD = 16
DOWN, UP = 0, 1
CURVE = math.sqrt(2.0 / math.pi)


def by_rows(left, right):
    return lax.dot_general(left, right, (((1,), (1,)), ((), ())), preferred_element_type=F32)


def by_cols(left, right):
    return lax.dot_general(left, right, (((0,), (0,)), ((), ())), preferred_element_type=F32)


def times(left, right):
    return jnp.dot(left, right, preferred_element_type=F32)


def lane_mask(shift):
    row = lax.broadcasted_iota(jnp.int32, (ROWS, 128), 0)
    lane = lax.broadcasted_iota(jnp.int32, (ROWS, 128), 1)
    return lane == row + shift


def to_lanes(column, shift):
    return jnp.sum(jnp.where(lane_mask(shift), column, 0.0), 0, keepdims=True)


def to_column(lanes, shift):
    return jnp.sum(jnp.where(lane_mask(shift), lanes, 0.0), 1, keepdims=True)


def spread_matrix(shards, unit):
    shape = (shards * unit, shards * PAD)
    row = lax.broadcasted_iota(jnp.int32, shape, 0)
    col = lax.broadcasted_iota(jnp.int32, shape, 1)
    shard = jnp.zeros(shape, jnp.int32)
    for k in range(1, shards):
        shard += jnp.where(row >= k * unit, 1, 0)
    return jnp.where(col == shard * PAD + row - shard * unit, 1.0, 0.0)


def relay_kernel(
    nz, copies, entry, exit_codes, exit_scale, slots, gain_ref, shard,
    sent, returned, grad_down, grad_up,
    zbuf, wv, span_src, span_in, spans, incf, incb, xs, norm_stat, scaled, pres, hidden, gsum,
    p1s, p1r, t1s, t1r, p2s, p2r, t2s, t2r, u1s, u1r, u2s, u2r,
    gs, gb, dpre_s, dxb, peak_src, peak_in, gp, rx1, rx2, zs, rz,
    span_sem, zsend, zrecv, xsend, xrecv, l1send, l1recv, l2send, l2recv,
    b1send, b1recv, b2send, b2recv, ysend, yrecv, wsend, wrecv, peak_sem,
    gxsend, gxrecv, gzsend, gzrecv,
):
    sec = lax.axis_index("section")
    last = lax.axis_size("section") - 1
    dp = lax.axis_index("dp")
    ten = lax.axis_index("tensor")
    x = dp // nz
    z = dp % nz
    half_z = nz // 2
    unit = grad_down.shape[0]
    cols = gain_ref.shape[1]
    half = cols // 2
    bot = pres.shape[2]
    total = cols * 4
    xr, xl, xo = (x + 1) % NX, (x + NX - 1) % NX, (x + 2) % NX
    to_right = {"dp": xr * nz + z}
    to_left = {"dp": xl * nz + z}
    mate = {"tensor": ten + 1 - 2 * (ten % 2)}
    far = {"tensor": (ten + 2) % 4}
    others = [{"tensor": (ten + k) % 4} for k in (1, 2, 3)]
    next_sec = {"section": (sec + 1) % (last + 1)}
    prev_sec = {"section": (sec + last) % (last + 1)}
    z_up = {"dp": x * nz + (z + 1) % nz}
    z_down = {"dp": x * nz + (z + nz - 1) % nz}

    barrier = pltpu.get_barrier_semaphore()
    friends = others + [next_sec, prev_sec, to_right, to_left, z_up, z_down]
    for friend in friends:
        pl.semaphore_signal(barrier, inc=1, device_id=friend, device_id_type=MESH)
    pl.semaphore_wait(barrier, len(friends))

    def move(src, dst, send, recv, device):
        return pltpu.make_async_remote_copy(
            src_ref=src, dst_ref=dst, send_sem=send, recv_sem=recv,
            device_id=device, device_id_type=MESH,
        )

    def z_move(way, slot, m):
        return move(
            zbuf.at[slot, m], zbuf.at[slot, m], zsend.at[way, slot, m], zrecv.at[slot, m],
            z_up if way == 0 else z_down,
        )

    def z_step(k):
        for m in (DOWN, UP):
            @pl.when(z - k >= 0)
            def _():
                z_move(0, z - k, m).wait_recv()

                @pl.when(z < nz - 1)
                def _():
                    z_move(0, z - k, m).start()

            @pl.when(z + k < nz)
            def _():
                z_move(1, z + k, m).wait_recv()

                @pl.when(z > 0)
                def _():
                    z_move(1, z + k, m).start()

    def z_steps(first, end):
        def step(k, carry):
            z_step(k)
            return carry

        lax.fori_loop(first, end, step, 0)

    group = [z // half_z, 1 - z // half_z]

    def x_move(p, m, kind):
        g = group[p]
        block, device, part = {
            0: (x, to_right, slice(None)),
            1: (x, to_left, slice(None)),
            2: (xl, to_right, slice(0, half)),
            3: (xr, to_left, slice(half, cols)),
        }[kind]
        ref = wv.at[m, block, g] if kind < 2 else wv.at[m, block, g, :, part]
        return move(ref, ref, xsend.at[p, m, kind], xrecv.at[p, m, kind], device)

    def x_arrival(p, m, kind):
        g = group[p]
        ref = {
            0: lambda: wv.at[m, xl, g],
            1: lambda: wv.at[m, xr, g],
            2: lambda: wv.at[m, xo, g, :, slice(0, half)],
            3: lambda: wv.at[m, xo, g, :, slice(half, cols)],
        }[kind]()
        move(ref, ref, xsend.at[p, m, kind], xrecv.at[p, m, kind], to_right).wait_recv()

    def x_own(p, m):
        block = zbuf[pl.ds(group[p] * half_z, half_z), m].reshape(half_z * PAD, cols)
        pick = spread_matrix(half_z, unit).astype(BF16)
        wv[m, x, group[p]] = times(pick, block).astype(BF16)
        x_move(p, m, 0).start()
        x_move(p, m, 1).start()

    def x_forward(p, m):
        x_arrival(p, m, 0)
        x_move(p, m, 2).start()
        x_arrival(p, m, 1)
        x_move(p, m, 3).start()

    def x_finish(p, m):
        x_arrival(p, m, 2)
        x_arrival(p, m, 3)

    zbuf[z] = shard[...]

    for m in (DOWN, UP):
        @pl.when(z < nz - 1)
        def _():
            z_move(0, z, m).start()

        @pl.when(z > 0)
        def _():
            z_move(1, z, m).start()

    @pl.when(sec == 0)
    def _():
        incf[...] = entry[...]

    def squares(m, carry):
        sums = []
        for k in range(2):
            rows = copies[k, slots[m]].astype(F32)
            sums.append(to_lanes(jnp.sum(rows * rows, 1, keepdims=True), m * ROWS))
        return carry[0] + sums[0], carry[1] + sums[1]

    nothing = jnp.zeros((1, 128), F32)
    square_in, square_out = lax.fori_loop(0, MICRO, squares, (nothing, nothing))
    span_src[...] = jnp.zeros((8, 128), F32)
    span_src[0:1] = square_in
    span_src[1:2] = square_out

    def span_move(k):
        return move(span_src, span_in.at[k], span_sem.at[0, k], span_sem.at[1, k], others[k])

    for k in range(3):
        span_move(k).start()

    z_steps(1, half_z)
    for m in (DOWN, UP):
        x_own(0, m)
    z_steps(half_z, half_z + 2)
    x_forward(0, DOWN)
    z_steps(half_z + 2, half_z + 3)
    x_forward(0, UP)
    z_steps(half_z + 3, nz)
    for m in (DOWN, UP):
        x_own(1, m)
    for k in range(3):
        span_move(k).wait_recv()
    spans[...] = 2.0 * jnp.sqrt(
        (span_src[...] + span_in[0] + span_in[1] + span_in[2]) / total + 1e-05
    )
    for m in (DOWN, UP):
        x_forward(1, m)
    x_finish(0, DOWN)
    x_finish(1, DOWN)

    def weights(m):
        return wv[m].reshape(bot, cols)

    gain = gain_ref[...]
    first = gain.astype(BF16).astype(F32)
    second = (gain - first).astype(BF16).astype(F32)
    third = gain - first - second
    row = lax.broadcasted_iota(jnp.int32, (PAD, cols), 0)
    terms = jnp.where(
        row == 0, first, jnp.where(row == 1, second, jnp.where(row == 2, third, 0.0))
    ).astype(BF16)
    gain_down = jnp.sum(by_rows(terms, weights(DOWN)), 0, keepdims=True)
    pieces = bot // 128

    def put_stat(ref, m, mean, spread, gd):
        ref[m] = jnp.zeros((8, 128), F32)
        ref[m, 0:1] = to_lanes(mean, 0)
        ref[m, 1:2] = to_lanes(spread, 0)
        for i in range(pieces):
            ref[m, 2 + i : 3 + i] = gd[:, i * 128 : (i + 1) * 128]

    def get_stat(ref, m):
        gd = jnp.concatenate([ref[m, 2 + i : 3 + i] for i in range(pieces)], axis=1)
        return to_column(ref[m, 0:1], 0), to_column(ref[m, 1:2], 0), gd

    def join(count, p, mean, spread, gd, p_other, mean_other, spread_other, gd_other):
        both = 0.5 * (mean + mean_other)
        mine, theirs = mean - both, mean_other - both
        spread_both = spread + spread_other + count * (mine * mine + theirs * theirs)
        p_both = (p + p_other) + (mine * gd + theirs * gd_other)
        return p_both, both, spread_both, gd + gd_other

    def l1(m):
        return (
            move(p1s.at[m], p1r.at[m], l1send.at[m, 0], l1recv.at[m, 0], mate),
            move(t1s.at[m], t1r.at[m], l1send.at[m, 1], l1recv.at[m, 1], mate),
        )

    def l2(m):
        return (
            move(p2s.at[m], p2r.at[m], l2send.at[m, 0], l2recv.at[m, 0], far),
            move(t2s.at[m], t2r.at[m], l2send.at[m, 1], l2recv.at[m, 1], far),
        )

    def y_forward(m):
        return move(sent.at[m], incf.at[m], ysend.at[m], yrecv.at[m], next_sec)

    def y_back(m):
        return move(dxb.at[m], incb.at[m], wsend.at[m], wrecv.at[m], prev_sec)

    def forward_in(m):
        @pl.when(sec > 0)
        def _():
            y_forward(m).wait_recv()

        span = to_column(spans[0:1], m * ROWS)
        rows = copies[0, slots[m]].astype(F32) + span * incf[m].astype(F32)
        xs[m] = rows
        mean = jnp.sum(rows, 1, keepdims=True) / cols
        centred = rows - mean
        spread = jnp.sum(centred * centred, 1, keepdims=True)
        part = by_rows((centred * gain_ref[...]).astype(BF16), weights(DOWN))
        p1s[m] = part
        put_stat(t1s, m, mean, spread, gain_down)
        for copy in l1(m):
            copy.start()
        for copy in l1(m):
            copy.wait_recv()
        part, mean, spread, gd = join(
            float(cols), part, mean, spread, gain_down, p1r[m], *get_stat(t1r, m)
        )
        p2s[m] = part.astype(BF16)
        put_stat(t2s, m, mean, spread, gd)
        for copy in l2(m):
            copy.start()

    def forward_out(m):
        for copy in l2(m):
            copy.wait_recv()
        raw, mean, spread, gd = join(
            float(2 * cols), p2s[m].astype(F32), *get_stat(t2s, m),
            p2r[m].astype(F32), *get_stat(t2r, m)
        )
        inverse = lax.rsqrt(spread / total + 1e-05)
        pre = raw * inverse
        gsum[...] = gd
        pres[m] = pre
        norm_stat[m, 0] = mean
        norm_stat[m, 1] = inverse
        act = (0.5 * pre * (1.0 + jnp.tanh(CURVE * (pre + 0.044715 * (pre * pre * pre))))).astype(BF16)
        hidden[m] = act
        result = xs[m] + times(act, weights(UP))
        span = to_column(spans[1:2], m * ROWS)
        sent[m] = jnp.clip(
            (result - copies[1, slots[m]].astype(F32)) / span, -1.0, 1.0
        ).astype(BF16)

        @pl.when(sec < last)
        def _():
            y_forward(m).start()

        scaled[m] = ((xs[m] - mean) * inverse * gain_ref[...]).astype(BF16)

    def forward_tick(i, carry):
        @pl.when(i < MICRO)
        def _():
            forward_in(i)

        @pl.when(i == 1)
        def _():
            x_finish(0, UP)
            x_finish(1, UP)

        @pl.when(i >= 1)
        def _():
            forward_out(i - 1)

        return carry

    lax.fori_loop(0, MICRO + 1, forward_tick, 0)

    def b1(m):
        return move(u1s.at[m], u1r.at[m], b1send.at[m], b1recv.at[m], mate)

    def b2(m):
        return move(u2s.at[m], u2r.at[m], b2send.at[m], b2recv.at[m], far)

    def backward_in(m):
        @pl.when(sec == last)
        def _():
            gs[m] = exit_codes[m].astype(F32) * exit_scale[m]

        @pl.when(sec < last)
        def _():
            y_back(m).wait_recv()
            gs[m] = incb[m].astype(F32)

        rounded = gs[m].astype(BF16)
        gb[m] = rounded
        part = by_rows(rounded, weights(UP))
        u1s[m] = part
        b1(m).start()
        b1(m).wait_recv()
        u2s[m] = (part + u1r[m]).astype(BF16)
        b2(m).start()

    def backward_out(m):
        b2(m).wait_recv()
        grad_act = u2s[m].astype(F32) + u2r[m].astype(F32)
        pre = pres[m]
        bend = jnp.tanh(CURVE * (pre + 0.044715 * (pre * pre * pre)))
        slope = 0.5 * (1.0 + bend) + 0.5 * pre * (1.0 - bend * bend) * (
            CURVE * (1.0 + 3.0 * 0.044715 * pre * pre)
        )
        dpre = (grad_act * slope).astype(BF16)
        dpre_s[m] = dpre
        wide = dpre.astype(F32)
        mean_grad = jnp.sum(wide * gsum[...], 1, keepdims=True) / total
        mean_cross = jnp.sum(wide * pre, 1, keepdims=True) / total
        mean, inverse = norm_stat[m, 0], norm_stat[m, 1]
        normed = (xs[m] - mean) * inverse
        dn = times(dpre, weights(DOWN)) * gain_ref[...]
        dx = gs[m] + inverse * (dn - mean_grad - normed * mean_cross)
        gs[m] = dx
        dxb[m] = dx.astype(BF16)

        @pl.when(sec > 0)
        def _():
            y_back(m).start()

        return to_lanes(jnp.max(jnp.abs(dx), 1, keepdims=True), m * ROWS)

    peak_src[...] = jnp.zeros((8, 128), F32)

    def backward_tick(i, carry):
        backward_in(i)

        @pl.when(i >= 1)
        def _():
            peak_src[0:1] += backward_out(i - 1)

        return carry

    lax.fori_loop(0, MICRO, backward_tick, 0)

    def gradient(m, left, right):
        width = 256
        lhs = left[...].reshape(MICRO * ROWS, bot)

        def tile(i, carry):
            at = pl.ds(pl.multiple_of(i * width, width), width)
            rhs = right[:, :, at].reshape(MICRO * ROWS, width)
            gp[m, :, :, at] = by_cols(lhs, rhs).astype(BF16).reshape(NX, bot // NX, width)
            return carry

        lax.fori_loop(0, cols // width, tile, 0)

    low, high = slice(0, half), slice(half, cols)

    def gx_move(m, kind):
        src, dst, device = {
            0: (gp.at[m, xo, :, low], rx1.at[m, 0], to_right),
            1: (gp.at[m, xo, :, high], rx1.at[m, 1], to_left),
            2: (gp.at[m, xr, :, high], rx2.at[m, 0, :, high], to_right),
            3: (gp.at[m, xl, :, low], rx2.at[m, 1, :, low], to_left),
            4: (gp.at[m, xr, :, low], rx2.at[m, 0, :, low], to_right),
            5: (gp.at[m, xl, :, high], rx2.at[m, 1, :, high], to_left),
        }[kind]
        return move(src, dst, gxsend.at[m, kind], gxrecv.at[m, kind], device)

    def scatter_start(m):
        for kind in range(4):
            gx_move(m, kind).start()

    def scatter_forward(m):
        gx_move(m, 0).wait_recv()
        gp[m, xr, :, low] = (gp[m, xr, :, low].astype(F32) + rx1[m, 0].astype(F32)).astype(BF16)
        gx_move(m, 4).start()
        gx_move(m, 1).wait_recv()
        gp[m, xl, :, high] = (gp[m, xl, :, high].astype(F32) + rx1[m, 1].astype(F32)).astype(BF16)
        gx_move(m, 5).start()

    def scatter_sum(m):
        for kind in range(2, 6):
            gx_move(m, kind).wait_recv()
        own = gp[m, x].astype(F32) + rx2[m, 0].astype(F32) + rx2[m, 1].astype(F32)
        pick = spread_matrix(nz, unit).astype(BF16)
        zs[m] = by_cols(pick, own.astype(BF16)).astype(BF16).reshape(nz, PAD, cols)

    def gz_move(m, way, target):
        return move(
            zs.at[m, target], rz.at[m, way, target], gzsend.at[m, target],
            gzrecv.at[m, way, target], z_up if way == 0 else z_down,
        )

    def chain_step(k, carry):
        for m in (UP, DOWN):
            for way, target, wanted, fed in (
                (0, nz - 1 - k, nz - 1 - k > z, z > 0),
                (1, k, k < z, z < nz - 1),
            ):
                @pl.when(wanted)
                def _():
                    @pl.when(fed)
                    def _():
                        gz_move(m, way, target).wait_recv()
                        zs[m, target] = (
                            zs[m, target].astype(F32) + rz[m, way, target].astype(F32)
                        ).astype(BF16)

                    gz_move(m, way, target).start()

        return carry

    gradient(UP, hidden, gb)
    scatter_start(UP)
    peak_src[0:1] += backward_out(MICRO - 1)

    def peak_move(k):
        return move(peak_src, peak_in.at[k], peak_sem.at[0, k], peak_sem.at[1, k], others[k])

    for k in range(3):
        peak_move(k).start()
    gradient(DOWN, dpre_s, scaled)
    scatter_start(DOWN)
    scatter_forward(UP)
    scatter_forward(DOWN)
    scatter_sum(UP)
    scatter_sum(DOWN)
    lax.fori_loop(0, nz - 1, chain_step, 0)

    for k in range(3):
        peak_move(k).wait_recv()
    peak_row = jnp.maximum(
        jnp.maximum(peak_src[0:1], peak_in[0, 0:1]),
        jnp.maximum(peak_in[1, 0:1], peak_in[2, 0:1]),
    )
    peak_row = (peak_row + 1e-05).astype(BF16).astype(F32)

    def codes_back(m, carry):
        returned[m] = (gs[m] / to_column(peak_row, m * ROWS)).astype(BF16)
        return carry

    lax.fori_loop(0, MICRO, codes_back, 0)

    for m, out in ((UP, grad_up), (DOWN, grad_down)):
        out[...] = zs[m, z, 0:unit].astype(F32)
        for way, fed in ((0, z > 0), (1, z < nz - 1)):
            @pl.when(fed)
            def _():
                gz_move(m, way, z).wait_recv()
                out[...] += rz[m, way, z, 0:unit].astype(F32)

    for k in range(3):
        span_move(k).wait_send()
        peak_move(k).wait_send()

    def drain_micro(m, carry):
        for copy in l1(m) + l2(m) + (b1(m), b2(m)):
            copy.wait_send()

        @pl.when(sec < last)
        def _():
            y_forward(m).wait_send()

        @pl.when(sec > 0)
        def _():
            y_back(m).wait_send()

        return carry

    lax.fori_loop(0, MICRO, drain_micro, 0)

    for m in (DOWN, UP):
        for p in range(2):
            for kind in range(4):
                x_move(p, m, kind).wait_send()
        for kind in range(6):
            gx_move(m, kind).wait_send()

    def drain_z(slot, carry):
        for m in (DOWN, UP):
            @pl.when((z < nz - 1) & (slot <= z))
            def _():
                z_move(0, slot, m).wait_send()

            @pl.when((z > 0) & (slot >= z))
            def _():
                z_move(1, slot, m).wait_send()

            @pl.when(slot > z)
            def _():
                gz_move(m, 0, slot).wait_send()

            @pl.when(slot < z)
            def _():
                gz_move(m, 1, slot).wait_send()

        return carry

    lax.fori_loop(0, nz, drain_z, 0)


def solution(mesh):
    nz = mesh.shape["dp"] // NX

    def local(stored, entry, exit_codes, exit_scales, slot_ids, gain, down, up):
        unit, cols = down.shape[1], down.shape[2]
        bot = unit * mesh.shape["dp"]
        tokens = MICRO * ROWS
        pad = lambda w: jnp.pad(w, ((0, PAD - unit), (0, 0)))
        shard = jnp.stack([pad(down[0]), pad(up[0])])
        block = (MICRO, ROWS, cols)
        small = (MICRO, ROWS, bot)
        dma = pltpu.SemaphoreType.DMA
        vm = pltpu.VMEM
        xrows = bot // NX
        scratch = [
            vm((nz, 2, PAD, cols), BF16),
            vm((2, NX, 2, xrows // 2, cols), BF16),
            vm((8, 128), F32), vm((3, 8, 128), F32), vm((8, 128), F32),
            vm(block, BF16), vm(block, BF16),
            vm(block, F32),
            vm((MICRO, 2, ROWS, 1), F32),
            vm(block, BF16),
            vm(small, F32), vm(small, BF16),
            vm((1, bot), F32),
            vm(small, F32), vm(small, F32), vm((MICRO, 8, 128), F32), vm((MICRO, 8, 128), F32),
            vm(small, BF16), vm(small, BF16), vm((MICRO, 8, 128), F32), vm((MICRO, 8, 128), F32),
            vm(small, F32), vm(small, F32), vm(small, BF16), vm(small, BF16),
            vm(block, F32), vm(block, BF16), vm(small, BF16), vm(block, BF16),
            vm((8, 128), F32), vm((3, 8, 128), F32),
            vm((2, NX, xrows, cols), BF16),
            vm((2, 2, xrows, cols // 2), BF16),
            vm((2, 2, xrows, cols), BF16),
            vm((2, nz, PAD, cols), BF16),
            vm((2, 2, nz, PAD, cols), BF16),
            dma((2, 3)),
            dma((2, nz, 2)), dma((nz, 2)),
            dma((2, 2, 4)), dma((2, 2, 4)),
            dma((MICRO, 2)), dma((MICRO, 2)), dma((MICRO, 2)), dma((MICRO, 2)),
            dma((MICRO,)), dma((MICRO,)), dma((MICRO,)), dma((MICRO,)),
            dma((MICRO,)), dma((MICRO,)), dma((MICRO,)), dma((MICRO,)),
            dma((2, 3)),
            dma((2, 6)), dma((2, 6)),
            dma((2, nz)), dma((2, 2, nz)),
        ]
        in_vmem = pl.BlockSpec(memory_space=pltpu.VMEM)
        sent, returned, grad_down, grad_up = pl.pallas_call(
            lambda *refs: relay_kernel(nz, *refs),
            out_shape=(
                jax.ShapeDtypeStruct(block, BF16),
                jax.ShapeDtypeStruct(block, BF16),
                jax.ShapeDtypeStruct((unit, cols), F32),
                jax.ShapeDtypeStruct((unit, cols), F32),
            ),
            in_specs=[in_vmem] * 4 + [pl.BlockSpec(memory_space=pltpu.SMEM)] + [in_vmem] * 2,
            out_specs=(in_vmem,) * 4,
            scratch_shapes=scratch,
            compiler_params=pltpu.CompilerParams(
                collective_id=0, has_side_effects=True, vmem_limit_bytes=48 * 2**20
            ),
        )(
            stored[0].reshape(2, MICRO, ROWS, cols),
            entry.reshape(block),
            exit_codes.reshape(block),
            exit_scales.reshape(MICRO, ROWS, 1),
            slot_ids[0],
            gain,
            shard,
        )
        return (
            sent.reshape(1, tokens, cols),
            returned.reshape(1, tokens, cols),
            grad_down[None],
            grad_up[None],
        )

    in_specs = (
        P("section", None, "dp", "tensor"),
        P("dp", "tensor"),
        P("dp", "tensor"),
        P("dp"),
        P("dp", None),
        P("section", "tensor"),
        P("section", "dp", "tensor"),
        P("section", "dp", "tensor"),
    )
    out_specs = (P("section", "dp", "tensor"),) * 4
    return jax.shard_map(local, mesh=mesh, in_specs=in_specs, out_specs=out_specs, check_vma=False)
```

time: 1950 us -> 378 us (0.19)
  the two profiles are of different devices: /device:TPU:6 before, /device:TPU:66 now
where the time goes in v1:
time: 378 us
  Pallas kernels  367 us (97%)
  local copies, waits for them, and re-layouts  9.69 us (3%)
    pallas_call x1, Pallas kernels, local(): pl.pallas_call(lambda *refs: relay_kernel(nz, *refs), out_shape=(jax.Shap...  367 us
    unnamed x14, local copies, waits for them, and re-layouts  7.89 us

profile of v1, /device:TPU:66, one launch (start us, length us, event | category | flops | bytes accessed | tf_op | source)
XLA Modules:
  0.0 377.9 jit_solution(13404315401462705694)
XLA Ops:
  0.6 0.9 reshape.28.refs_3_
  1.5 0.9 pad_bitcast_fusion
  2.5 0.0 copy-start
  2.5 1.3 copy-done
  3.7 0.0 copy-start.1
  3.7 1.1 copy-done.1
  4.8 0.0 copy-start.2
  4.8 1.1 copy-done.2
  5.9 0.0 copy-start.3
  5.9 0.7 copy-done.3
  6.6 0.0 copy-start.4
  6.6 0.7 copy-done.4
  7.2 367.5 %shard_map.111 = (bf16[4,32,2304]{2,1,0:T(8,128)(2,1)S(1)}, bf16[4,32,2304]{2,1,0:T(8,128)(2,1)S(1)}, f32[12,2304]{1,0:T(8,128)S(1)}, f32[12,2304]{1,0:T(8,128)S(1)}) custom-call(bf16[2,4,32,2304]{3,2,1,0:T(8,128)(2,1)S(1)} %bitcast.14, bf16[4,32,2304]{2,1,0:T(8,128)(2,1)S(1)} %bitcast.17, bf16[4,32,2304]{2,1,0:T(8,128)(2,1)S(1)} %bitcast.18, ...), custom_call_target="tpu_custom_call" | custom-call | tf_op jit(solution)/shard_map/pallas_call | solution.py:615
  374.7 0.8 copy.13
  375.5 0.8 copy.14
  376.2 0.8 copy.17
  377.0 0.8 copy.18
  (1 shorter events, 0.0 us)
Async XLA Ops:
  2.5 1.3 copy-start
  3.7 1.1 copy-start.1
  4.8 1.1 copy-start.2
  5.9 0.7 copy-start.3
  6.6 0.7 copy-start.4

commit v2 on v1

--- a/solution.py
+++ b/solution.py
@@ -57,12 +57,12 @@
 def relay_kernel(
     nz, copies, entry, exit_codes, exit_scale, slots, gain_ref, shard,
     sent, returned, grad_down, grad_up,
-    zbuf, wv, span_src, span_in, spans, incf, incb, xs, norm_stat, scaled, pres, hidden, gsum,
+    zbuf, wv, span_src, span_in, spans, incf, incb, xs, norm_stat, pres, gsum,
     p1s, p1r, t1s, t1r, p2s, p2r, t2s, t2r, u1s, u1r, u2s, u2r,
-    gs, gb, dpre_s, dxb, peak_src, peak_in, gp, rx1, rx2, zs, rz,
+    gs, dxb, peak_src, peak_in, scaled, hidden, gb, dpre_s, pair_out, pair_in, own, zs, rz,
     span_sem, zsend, zrecv, xsend, xrecv, l1send, l1recv, l2send, l2recv,
     b1send, b1recv, b2send, b2recv, ysend, yrecv, wsend, wrecv, peak_sem,
-    gxsend, gxrecv, gzsend, gzrecv,
+    fsend, frecv, psend, precv, gzsend, gzrecv,
 ):
     sec = lax.axis_index("section")
     last = lax.axis_size("section") - 1
@@ -88,7 +88,10 @@
     z_down = {"dp": x * nz + (z + nz - 1) % nz}
 
     barrier = pltpu.get_barrier_semaphore()
-    friends = others + [next_sec, prev_sec, to_right, to_left, z_up, z_down]
+    x_peers = [{"dp": (x + k) % NX * nz + z} for k in (1, 2, 3)]
+    z_peers = [{"dp": x * nz + (z + 2 * k) % nz} for k in (1, 2, 3)]
+    z_mate = {"dp": dp + 1 - 2 * (z % 2)}
+    friends = others + [next_sec, prev_sec, z_up, z_down] + x_peers + z_peers
     for friend in friends:
         pl.semaphore_signal(barrier, inc=1, device_id=friend, device_id_type=MESH)
     pl.semaphore_wait(barrier, len(friends))
@@ -274,6 +277,31 @@
     def y_back(m):
         return move(dxb.at[m], incb.at[m], wsend.at[m], wrecv.at[m], prev_sec)
 
+    def each(step):
+        def tick(m, carry):
+            step(m)
+            return carry
+
+        lax.fori_loop(0, MICRO, tick, 0)
+
+    factors = (scaled, hidden, gb, dpre_s)
+
+    def factor_move(which, m, k):
+        ref = factors[which].at[x, m]
+        return move(ref, ref, fsend.at[which, m, k], frecv.at[which, m, k], x_peers[k])
+
+    def factor_send(which, m):
+        for k in range(3):
+            factor_move(which, m, k).start()
+
+    def factor_wait(which):
+        def wait(m):
+            for k in range(3):
+                ref = factors[which].at[(x + NX - 1 - k) % NX, m]
+                move(ref, ref, fsend.at[which, m, k], frecv.at[which, m, k], x_peers[k]).wait_recv()
+
+        each(wait)
+
     def forward_in(m):
         @pl.when(sec > 0)
         def _():
@@ -314,7 +342,7 @@
         norm_stat[m, 0] = mean
         norm_stat[m, 1] = inverse
         act = (0.5 * pre * (1.0 + jnp.tanh(CURVE * (pre + 0.044715 * (pre * pre * pre))))).astype(BF16)
-        hidden[m] = act
+        hidden[x, m] = act
         result = xs[m] + times(act, weights(UP))
         span = to_column(spans[1:2], m * ROWS)
         sent[m] = jnp.clip(
@@ -325,25 +353,9 @@
         def _():
             y_forward(m).start()
 
-        scaled[m] = ((xs[m] - mean) * inverse * gain_ref[...]).astype(BF16)
-
-    def forward_tick(i, carry):
-        @pl.when(i < MICRO)
-        def _():
-            forward_in(i)
-
-        @pl.when(i == 1)
-        def _():
-            x_finish(0, UP)
-            x_finish(1, UP)
-
-        @pl.when(i >= 1)
-        def _():
-            forward_out(i - 1)
-
-        return carry
-
-    lax.fori_loop(0, MICRO + 1, forward_tick, 0)
+        scaled[x, m] = ((xs[m] - mean) * inverse * gain_ref[...]).astype(BF16)
+        factor_send(0, m)
+        factor_send(1, m)
 
     def b1(m):
         return move(u1s.at[m], u1r.at[m], b1send.at[m], b1recv.at[m], mate)
@@ -362,13 +374,14 @@
             gs[m] = incb[m].astype(F32)
 
         rounded = gs[m].astype(BF16)
-        gb[m] = rounded
+        gb[x, m] = rounded
         part = by_rows(rounded, weights(UP))
         u1s[m] = part
         b1(m).start()
         b1(m).wait_recv()
         u2s[m] = (part + u1r[m]).astype(BF16)
         b2(m).start()
+        factor_send(2, m)
 
     def backward_out(m):
         b2(m).wait_recv()
@@ -379,7 +392,8 @@
             CURVE * (1.0 + 3.0 * 0.044715 * pre * pre)
         )
         dpre = (grad_act * slope).astype(BF16)
-        dpre_s[m] = dpre
+        dpre_s[x, m] = dpre
+        factor_send(3, m)
         wide = dpre.astype(F32)
         mean_grad = jnp.sum(wide * gsum[...], 1, keepdims=True) / total
         mean_cross = jnp.sum(wide * pre, 1, keepdims=True) / total
@@ -394,106 +408,100 @@
         def _():
             y_back(m).start()
 
-        return to_lanes(jnp.max(jnp.abs(dx), 1, keepdims=True), m * ROWS)
+        peak_src[0:1] += to_lanes(jnp.max(jnp.abs(dx), 1, keepdims=True), m * ROWS)
 
     peak_src[...] = jnp.zeros((8, 128), F32)
 
-    def backward_tick(i, carry):
-        backward_in(i)
-
-        @pl.when(i >= 1)
-        def _():
-            peak_src[0:1] += backward_out(i - 1)
-
-        return carry
-
-    lax.fori_loop(0, MICRO, backward_tick, 0)
-
-    def gradient(m, left, right):
-        width = 256
-        lhs = left[...].reshape(MICRO * ROWS, bot)
-
-        def tile(i, carry):
-            at = pl.ds(pl.multiple_of(i * width, width), width)
-            rhs = right[:, :, at].reshape(MICRO * ROWS, width)
-            gp[m, :, :, at] = by_cols(lhs, rhs).astype(BF16).reshape(NX, bot // NX, width)
+    @pl.when(sec == last)
+    def _():
+        x_finish(0, UP)
+        x_finish(1, UP)
+        each(backward_in)
+
+    each(forward_in)
+
+    @pl.when(sec < last)
+    def _():
+        x_finish(0, UP)
+        x_finish(1, UP)
+
+    def forward_end(m):
+        forward_out(m)
+
+        @pl.when(sec == last)
+        def _():
+            backward_out(m)
+
+    each(forward_end)
+
+    @pl.when(sec < last)
+    def _():
+        each(backward_in)
+
+        def tick(m, carry):
+            backward_out(m)
             return carry
 
-        lax.fori_loop(0, cols // width, tile, 0)
-
-    low, high = slice(0, half), slice(half, cols)
-
-    def gx_move(m, kind):
-        src, dst, device = {
-            0: (gp.at[m, xo, :, low], rx1.at[m, 0], to_right),
-            1: (gp.at[m, xo, :, high], rx1.at[m, 1], to_left),
-            2: (gp.at[m, xr, :, high], rx2.at[m, 0, :, high], to_right),
-            3: (gp.at[m, xl, :, low], rx2.at[m, 1, :, low], to_left),
-            4: (gp.at[m, xr, :, low], rx2.at[m, 0, :, low], to_right),
-            5: (gp.at[m, xl, :, high], rx2.at[m, 1, :, high], to_left),
-        }[kind]
-        return move(src, dst, gxsend.at[m, kind], gxrecv.at[m, kind], device)
-
-    def scatter_start(m):
-        for kind in range(4):
-            gx_move(m, kind).start()
-
-    def scatter_forward(m):
-        gx_move(m, 0).wait_recv()
-        gp[m, xr, :, low] = (gp[m, xr, :, low].astype(F32) + rx1[m, 0].astype(F32)).astype(BF16)
-        gx_move(m, 4).start()
-        gx_move(m, 1).wait_recv()
-        gp[m, xl, :, high] = (gp[m, xl, :, high].astype(F32) + rx1[m, 1].astype(F32)).astype(BF16)
-        gx_move(m, 5).start()
-
-    def scatter_sum(m):
-        for kind in range(2, 6):
-            gx_move(m, kind).wait_recv()
-        own = gp[m, x].astype(F32) + rx2[m, 0].astype(F32) + rx2[m, 1].astype(F32)
-        pick = spread_matrix(nz, unit).astype(BF16)
-        zs[m] = by_cols(pick, own.astype(BF16)).astype(BF16).reshape(nz, PAD, cols)
-
-    def gz_move(m, way, target):
-        return move(
-            zs.at[m, target], rz.at[m, way, target], gzsend.at[m, target],
-            gzrecv.at[m, way, target], z_up if way == 0 else z_down,
-        )
-
-    def chain_step(k, carry):
-        for m in (UP, DOWN):
-            for way, target, wanted, fed in (
-                (0, nz - 1 - k, nz - 1 - k > z, z > 0),
-                (1, k, k < z, z < nz - 1),
-            ):
-                @pl.when(wanted)
-                def _():
-                    @pl.when(fed)
-                    def _():
-                        gz_move(m, way, target).wait_recv()
-                        zs[m, target] = (
-                            zs[m, target].astype(F32) + rz[m, way, target].astype(F32)
-                        ).astype(BF16)
-
-                    gz_move(m, way, target).start()
-
-        return carry
-
-    gradient(UP, hidden, gb)
-    scatter_start(UP)
-    peak_src[0:1] += backward_out(MICRO - 1)
+        lax.fori_loop(0, MICRO - 1, tick, 0)
+
+    quarter = nz // 2
+    parity = z % 2
+
+    def unit_pick(side):
+        shape = (bot, quarter * unit)
+        row = lax.broadcasted_iota(jnp.int32, shape, 0)
+        col = lax.broadcasted_iota(jnp.int32, shape, 1)
+        source = col + (x * nz + side) * unit
+        for k in range(1, quarter):
+            source += jnp.where(col >= k * unit, unit, 0)
+        return jnp.where(row == source, 1.0, 0.0).astype(BF16)
+
+    def gradient(p, side):
+        left, right = (hidden, gb) if p < 2 else (dpre_s, scaled)
+        tokens = NX * MICRO * ROWS
+        at = slice(p % 2 * half, (p % 2 + 1) * half)
+        lhs = times(left[...].reshape(tokens, bot), unit_pick(side)).astype(BF16)
+        return by_cols(lhs, right[:, :, :, at].reshape(tokens, half))
+
+    def pair_move(p):
+        return move(pair_out.at[p], pair_in.at[p], psend.at[p], precv.at[p], z_mate)
+
+    def gz_move(p, k):
+        slot = (z + 2 * (k + 1)) % nz // 2
+        return move(zs.at[p, slot], rz.at[p, k], gzsend.at[p, k], gzrecv.at[p, k], z_peers[k])
+
+    def gradient_first(pieces):
+        for p in pieces:
+            pair_out[p] = gradient(p, 1 - parity).astype(BF16)
+            pair_move(p).start()
+        for p in pieces:
+            own[p] = gradient(p, parity)
+
+    def gradient_second(p):
+        pair_move(p).wait_recv()
+        both = (own[p] + pair_in[p].astype(F32)).astype(BF16)
+        pad = spread_matrix(quarter, unit).astype(BF16)
+        zs[p] = by_cols(pad, both).astype(BF16).reshape(quarter, PAD, half)
+        for k in range(3):
+            gz_move(p, k).start()
+
+    @pl.when(sec < last)
+    def _():
+        backward_out(MICRO - 1)
 
     def peak_move(k):
         return move(peak_src, peak_in.at[k], peak_sem.at[0, k], peak_sem.at[1, k], others[k])
 
     for k in range(3):
         peak_move(k).start()
-    gradient(DOWN, dpre_s, scaled)
-    scatter_start(DOWN)
-    scatter_forward(UP)
-    scatter_forward(DOWN)
-    scatter_sum(UP)
-    scatter_sum(DOWN)
-    lax.fori_loop(0, nz - 1, chain_step, 0)
+    factor_wait(1)
+    factor_wait(2)
+    gradient_first((0, 1))
+    factor_wait(0)
+    factor_wait(3)
+    gradient_first((2, 3))
+    for p in range(4):
+        gradient_second(p)
 
     for k in range(3):
         peak_move(k).wait_recv()
@@ -503,19 +511,19 @@
     )
     peak_row = (peak_row + 1e-05).astype(BF16).astype(F32)
 
-    def codes_back(m, carry):
+    def codes_back(m):
         returned[m] = (gs[m] / to_column(peak_row, m * ROWS)).astype(BF16)
-        return carry
-
-    lax.fori_loop(0, MICRO, codes_back, 0)
-
-    for m, out in ((UP, grad_up), (DOWN, grad_down)):
-        out[...] = zs[m, z, 0:unit].astype(F32)
-        for way, fed in ((0, z > 0), (1, z < nz - 1)):
-            @pl.when(fed)
-            def _():
-                gz_move(m, way, z).wait_recv()
-                out[...] += rz[m, way, z, 0:unit].astype(F32)
+
+    each(codes_back)
+
+    for p in range(4):
+        out = grad_up if p < 2 else grad_down
+        at = slice(p % 2 * half, (p % 2 + 1) * half)
+        result = zs[p, z // 2].astype(F32)
+        for k in range(3):
+            gz_move(p, k).wait_recv()
+            result += rz[p, k].astype(F32)
+        out[:, at] = result[0:unit]
 
     for k in range(3):
         span_move(k).wait_send()
@@ -541,8 +549,18 @@
         for p in range(2):
             for kind in range(4):
                 x_move(p, m, kind).wait_send()
-        for kind in range(6):
-            gx_move(m, kind).wait_send()
+
+    for p in range(4):
+        pair_move(p).wait_send()
+        for k in range(3):
+            gz_move(p, k).wait_send()
+
+    def drain_factors(m):
+        for which in range(4):
+            for k in range(3):
+                factor_move(which, m, k).wait_send()
+
+    each(drain_factors)
 
     def drain_z(slot, carry):
         for m in (DOWN, UP):
@@ -553,14 +571,6 @@
             @pl.when((z > 0) & (slot >= z))
             def _():
                 z_move(1, slot, m).wait_send()
-
-            @pl.when(slot > z)
-            def _():
-                gz_move(m, 0, slot).wait_send()
-
-            @pl.when(slot < z)
-            def _():
-                gz_move(m, 1, slot).wait_send()
 
         return carry
 
@@ -588,19 +598,19 @@
             vm(block, BF16), vm(block, BF16),
             vm(block, F32),
             vm((MICRO, 2, ROWS, 1), F32),
-            vm(block, BF16),
-            vm(small, F32), vm(small, BF16),
+            vm(small, F32),
             vm((1, bot), F32),
             vm(small, F32), vm(small, F32), vm((MICRO, 8, 128), F32), vm((MICRO, 8, 128), F32),
             vm(small, BF16), vm(small, BF16), vm((MICRO, 8, 128), F32), vm((MICRO, 8, 128), F32),
             vm(small, F32), vm(small, F32), vm(small, BF16), vm(small, BF16),
-            vm(block, F32), vm(block, BF16), vm(small, BF16), vm(block, BF16),
+            vm(block, F32), vm(block, BF16),
             vm((8, 128), F32), vm((3, 8, 128), F32),
-            vm((2, NX, xrows, cols), BF16),
-            vm((2, 2, xrows, cols // 2), BF16),
-            vm((2, 2, xrows, cols), BF16),
-            vm((2, nz, PAD, cols), BF16),
-            vm((2, 2, nz, PAD, cols), BF16),
+            vm((NX, *block), BF16), vm((NX, *small), BF16),
+            vm((NX, *block), BF16), vm((NX, *small), BF16),
+            vm((4, xrows // 2, cols // 2), BF16), vm((4, xrows // 2, cols // 2), BF16),
+            vm((4, xrows // 2, cols // 2), F32),
+            vm((4, nz // 2, PAD, cols // 2), BF16),
+            vm((4, 3, PAD, cols // 2), BF16),
             dma((2, 3)),
             dma((2, nz, 2)), dma((nz, 2)),
             dma((2, 2, 4)), dma((2, 2, 4)),
@@ -608,8 +618,9 @@
             dma((MICRO,)), dma((MICRO,)), dma((MICRO,)), dma((MICRO,)),
             dma((MICRO,)), dma((MICRO,)), dma((MICRO,)), dma((MICRO,)),
             dma((2, 3)),
-            dma((2, 6)), dma((2, 6)),
-            dma((2, nz)), dma((2, 2, nz)),
+            dma((4, MICRO, 3)), dma((4, MICRO, 3)),
+            dma((4,)), dma((4,)),
+            dma((4, 3)), dma((4, 3)),
         ]
         in_vmem = pl.BlockSpec(memory_space=pltpu.VMEM)
         sent, returned, grad_down, grad_up = pl.pallas_call(

time: 378 us -> 236 us (0.62)
  the two profiles are of different devices: /device:TPU:66 before, /device:TPU:6 now
where the time goes in v2:
time: 236 us
  Pallas kernels  226 us (96%)
  local copies, waits for them, and re-layouts  9.69 us (4%)
    pallas_call x1, Pallas kernels, local(): pl.pallas_call(lambda *refs: relay_kernel(nz, *refs), out_shape=(jax.Shap...  226 us
    unnamed x14, local copies, waits for them, and re-layouts  7.89 us

profile of v2, /device:TPU:6, one launch (start us, length us, event | category | flops | bytes accessed | tf_op | source)
XLA Modules:
  0.0 236.0 jit_solution(17197063949145136595)
XLA Ops:
  0.6 0.9 reshape.28.refs_3_
  1.5 0.9 pad_bitcast_fusion
  2.5 0.0 copy-start
  2.5 1.3 copy-done
  3.7 0.0 copy-start.1
  3.7 1.1 copy-done.1
  4.8 0.0 copy-start.2
  4.8 1.1 copy-done.2
  5.9 0.0 copy-start.3
  5.9 0.7 copy-done.3
  6.6 0.0 copy-start.4
  6.6 0.7 copy-done.4
  7.2 225.6 %shard_map.111 = (bf16[4,32,2304]{2,1,0:T(8,128)(2,1)S(1)}, bf16[4,32,2304]{2,1,0:T(8,128)(2,1)S(1)}, f32[12,2304]{1,0:T(8,128)S(1)}, f32[12,2304]{1,0:T(8,128)S(1)}) custom-call(bf16[2,4,32,2304]{3,2,1,0:T(8,128)(2,1)S(1)} %bitcast.14, bf16[4,32,2304]{2,1,0:T(8,128)(2,1)S(1)} %bitcast.17, bf16[4,32,2304]{2,1,0:T(8,128)(2,1)S(1)} %bitcast.18, ...), custom_call_target="tpu_custom_call" | custom-call | tf_op jit(solution)/shard_map/pallas_call | solution.py:626
  232.8 0.8 copy.13
  233.6 0.8 copy.14
  234.3 0.8 copy.17
  235.2 0.8 copy.18
  (1 shorter events, 0.0 us)
Async XLA Ops:
  2.5 1.3 copy-start
  3.7 1.1 copy-start.1
  4.8 1.1 copy-start.2
  5.9 0.7 copy-start.3
  6.6 0.7 copy-start.4

commit v3 on v2

v3 whole, which is shorter than its diff:
```python
import math

import jax
import jax.numpy as jnp
from jax import lax
from jax.experimental import pallas as pl
from jax.experimental.pallas import tpu as pltpu
from jax.sharding import PartitionSpec as P

MESH = pl.DeviceIdType.MESH
F32 = jnp.float32
BF16 = jnp.bfloat16
MICRO = 4
ROWS = 32
NX = 4
PAD = 16
DOWN, UP, NEXT_DOWN, PREV_UP = ALL = (0, 1, 2, 3)
OWN, HOP = 0, 1
CURVE = math.sqrt(2.0 / math.pi)


def by_rows(left, right):
    return lax.dot_general(left, right, (((1,), (1,)), ((), ())), preferred_element_type=F32)


def by_cols(left, right):
    return lax.dot_general(left, right, (((0,), (0,)), ((), ())), preferred_element_type=F32)


def times(left, right):
    return jnp.dot(left, right, preferred_element_type=F32)


def lane_mask(shift):
    row = lax.broadcasted_iota(jnp.int32, (ROWS, 128), 0)
    lane = lax.broadcasted_iota(jnp.int32, (ROWS, 128), 1)
    return lane == row + shift


def to_lanes(column, shift):
    return jnp.sum(jnp.where(lane_mask(shift), column, 0.0), 0, keepdims=True)


def to_column(lanes, shift):
    return jnp.sum(jnp.where(lane_mask(shift), lanes, 0.0), 1, keepdims=True)


def spread_matrix(shards, unit):
    shape = (shards * unit, shards * PAD)
    row = lax.broadcasted_iota(jnp.int32, shape, 0)
    col = lax.broadcasted_iota(jnp.int32, shape, 1)
    shard = jnp.zeros(shape, jnp.int32)
    for k in range(1, shards):
        shard += jnp.where(row >= k * unit, 1, 0)
    return jnp.where(col == shard * PAD + row - shard * unit, 1.0, 0.0)


def relay_kernel(
    nz, copies, entry, exit_codes, exit_scale, slots, gain_ref, shard,
    sent, returned, grad_down, grad_up,
    zbuf, wv, span_src, span_in, spans, incf, incb, xs, norm_stat, pres, gsum,
    own_gain_down, next_gain_down, next_gain,
    p1s, p1r, t1s, t1r, p2s, p2r, t2s, t2r, u1s, u1r, u2s, u2r,
    gs, dxb, peak_src, peak_in, scaled, hidden, gb, dpre_s, pair_out, pair_in, own, zs, rz,
    span_sem, ssend, srecv, zsend, zrecv, xsend, xrecv, l1send, l1recv, l2send, l2recv,
    b1send, b1recv, b2send, b2recv, ysend, yrecv, wsend, wrecv, peak_sem,
    fsend, frecv, psend, precv, gzsend, gzrecv,
):
    sec = lax.axis_index("section")
    last = lax.axis_size("section") - 1
    dp = lax.axis_index("dp")
    ten = lax.axis_index("tensor")
    x = dp // nz
    z = dp % nz
    half_z = nz // 2
    unit = grad_down.shape[0]
    cols = gain_ref.shape[1]
    half = cols // 2
    bot = pres.shape[2]
    total = cols * 4
    xr, xl, xo = (x + 1) % NX, (x + NX - 1) % NX, (x + 2) % NX
    to_right = {"dp": xr * nz + z}
    to_left = {"dp": xl * nz + z}
    mate = {"tensor": ten + 1 - 2 * (ten % 2)}
    far = {"tensor": (ten + 2) % 4}
    others = [{"tensor": (ten + k) % 4} for k in (1, 2, 3)]
    next_sec = {"section": (sec + 1) % (last + 1)}
    prev_sec = {"section": (sec + last) % (last + 1)}
    z_up = {"dp": x * nz + (z + 1) % nz}
    z_down = {"dp": x * nz + (z + nz - 1) % nz}

    barrier = pltpu.get_barrier_semaphore()
    x_peers = [{"dp": (x + k) % NX * nz + z} for k in (1, 2, 3)]
    z_peers = [{"dp": x * nz + (z + 2 * k) % nz} for k in (1, 2, 3)]
    z_mate = {"dp": dp + 1 - 2 * (z % 2)}
    diagonal = [{"section": to["section"], "tensor": far["tensor"]} for to in (next_sec, prev_sec)]
    friends = others + [next_sec, prev_sec, z_up, z_down] + x_peers + z_peers + diagonal
    for friend in friends:
        pl.semaphore_signal(barrier, inc=1, device_id=friend, device_id_type=MESH)
    pl.semaphore_wait(barrier, len(friends))

    def move(src, dst, send, recv, device):
        return pltpu.make_async_remote_copy(
            src_ref=src, dst_ref=dst, send_sem=send, recv_sem=recv,
            device_id=device, device_id_type=MESH,
        )

    def each(step):
        def tick(m, carry):
            step(m)
            return carry

        lax.fori_loop(0, MICRO, tick, 0)

    has = {DOWN: None, UP: None, NEXT_DOWN: sec < last, PREV_UP: sec > 0}

    def if_has(m, step):
        if has[m] is None:
            step()
        else:
            pl.when(has[m])(step)

    def shard_move(m):
        if m == NEXT_DOWN:
            return move(shard.at[DOWN], zbuf.at[z, m], ssend.at[0], srecv.at[0], prev_sec)
        if m == PREV_UP:
            return move(shard.at[UP], zbuf.at[z, m], ssend.at[1], srecv.at[1], next_sec)
        return move(gain_ref, next_gain, ssend.at[2], srecv.at[2], prev_sec)

    def z_move(way, slot, m):
        return move(
            zbuf.at[slot, m], zbuf.at[slot, m], zsend.at[way, slot, m], zrecv.at[slot, m],
            z_up if way == 0 else z_down,
        )

    def z_begin(m):
        @pl.when(z < nz - 1)
        def _():
            z_move(0, z, m).start()

        @pl.when(z > 0)
        def _():
            z_move(1, z, m).start()

    def z_step(k):
        for m in ALL:
            def pass_on():
                @pl.when(z - k >= 0)
                def _():
                    z_move(0, z - k, m).wait_recv()

                    @pl.when(z < nz - 1)
                    def _():
                        z_move(0, z - k, m).start()

                @pl.when(z + k < nz)
                def _():
                    z_move(1, z + k, m).wait_recv()

                    @pl.when(z > 0)
                    def _():
                        z_move(1, z + k, m).start()

            if_has(m, pass_on)

    def z_steps(first, end):
        def step(k, carry):
            z_step(k)
            return carry

        lax.fori_loop(first, end, step, 0)

    group = [z // half_z, 1 - z // half_z]

    def x_move(p, m, kind):
        g = group[p]
        block, device, part = {
            0: (x, to_right, slice(None)),
            1: (x, to_left, slice(None)),
            2: (xl, to_right, slice(0, half)),
            3: (xr, to_left, slice(half, cols)),
        }[kind]
        ref = wv.at[m, block, g] if kind < 2 else wv.at[m, block, g, :, part]
        return move(ref, ref, xsend.at[p, m, kind], xrecv.at[p, m, kind], device)

    def x_arrival(p, m, kind):
        g = group[p]
        ref = {
            0: lambda: wv.at[m, xl, g],
            1: lambda: wv.at[m, xr, g],
            2: lambda: wv.at[m, xo, g, :, slice(0, half)],
            3: lambda: wv.at[m, xo, g, :, slice(half, cols)],
        }[kind]()
        move(ref, ref, xsend.at[p, m, kind], xrecv.at[p, m, kind], to_right).wait_recv()

    def x_own(p, m):
        block = zbuf[pl.ds(group[p] * half_z, half_z), m].reshape(half_z * PAD, cols)
        pick = spread_matrix(half_z, unit).astype(BF16)
        wv[m, x, group[p]] = times(pick, block).astype(BF16)
        x_move(p, m, 0).start()
        x_move(p, m, 1).start()

    def x_forward(p, m):
        x_arrival(p, m, 0)
        x_move(p, m, 2).start()
        x_arrival(p, m, 1)
        x_move(p, m, 3).start()

    def x_finish(m):
        for p in range(2):
            x_arrival(p, m, 2)
            x_arrival(p, m, 3)

    @pl.when(sec > 0)
    def _():
        shard_move(NEXT_DOWN).start()
        shard_move(None).start()

    @pl.when(sec < last)
    def _():
        shard_move(PREV_UP).start()

    for m in (DOWN, UP):
        zbuf[z, m] = shard[m]
        z_begin(m)

    def squares(m, carry):
        sums = []
        for k in range(2):
            rows = copies[k, slots[m]].astype(F32)
            sums.append(to_lanes(jnp.sum(rows * rows, 1, keepdims=True), m * ROWS))
        return carry[0] + sums[0], carry[1] + sums[1]

    nothing = jnp.zeros((1, 128), F32)
    square_in, square_out = lax.fori_loop(0, MICRO, squares, (nothing, nothing))
    span_src[...] = jnp.zeros((8, 128), F32)
    span_src[0:1] = square_in
    span_src[1:2] = square_out

    def span_move(k):
        return move(span_src, span_in.at[k], span_sem.at[0, k], span_sem.at[1, k], others[k])

    for k in range(3):
        span_move(k).start()

    @pl.when(sec < last)
    def _():
        shard_move(NEXT_DOWN).wait_recv()
        z_begin(NEXT_DOWN)

    @pl.when(sec > 0)
    def _():
        shard_move(PREV_UP).wait_recv()
        z_begin(PREV_UP)

    z_steps(1, half_z)
    for m in (DOWN, UP, NEXT_DOWN):
        if_has(m, lambda: x_own(0, m))
    z_steps(half_z, half_z + 2)
    x_forward(0, DOWN)
    z_steps(half_z + 2, half_z + 3)
    x_forward(0, UP)
    z_steps(half_z + 3, nz)
    for m in (DOWN, UP, NEXT_DOWN):
        if_has(m, lambda: x_own(1, m))
    if_has(NEXT_DOWN, lambda: x_forward(0, NEXT_DOWN))
    for p in range(2):
        if_has(PREV_UP, lambda: x_own(p, PREV_UP))
    for k in range(3):
        span_move(k).wait_recv()
    spans[...] = 2.0 * jnp.sqrt(
        (span_src[...] + span_in[0] + span_in[1] + span_in[2]) / total + 1e-05
    )
    x_forward(1, DOWN)
    x_forward(1, UP)
    x_finish(DOWN)

    def weights(m):
        return wv[m].reshape(bot, cols)

    def gain_times(gain, m):
        first = gain.astype(BF16).astype(F32)
        second = (gain - first).astype(BF16).astype(F32)
        third = gain - first - second
        row = lax.broadcasted_iota(jnp.int32, (PAD, cols), 0)
        terms = jnp.where(
            row == 0, first, jnp.where(row == 1, second, jnp.where(row == 2, third, 0.0))
        ).astype(BF16)
        return jnp.sum(by_rows(terms, weights(m)), 0, keepdims=True)

    pieces = bot // 128

    def put_stat(ref, mean, spread, gd):
        ref[...] = jnp.zeros((8, 128), F32)
        ref[0:1] = to_lanes(mean, 0)
        ref[1:2] = to_lanes(spread, 0)
        for i in range(pieces):
            ref[2 + i : 3 + i] = gd[:, i * 128 : (i + 1) * 128]

    def get_stat(ref):
        gd = jnp.concatenate([ref[2 + i : 3 + i] for i in range(pieces)], axis=1)
        return to_column(ref[0:1], 0), to_column(ref[1:2], 0), gd

    def join(count, p, mean, spread, gd, p_other, mean_other, spread_other, gd_other):
        both = 0.5 * (mean + mean_other)
        mine, theirs = mean - both, mean_other - both
        spread_both = spread + spread_other + count * (mine * mine + theirs * theirs)
        p_both = (p + p_other) + (mine * gd + theirs * gd_other)
        return p_both, both, spread_both, gd + gd_other

    far_of, far_before = diagonal

    def l1(step, m):
        return [
            move(src.at[step, m], dst.at[step, m], l1send.at[step, m, i], l1recv.at[step, m, i], mate)
            for i, (src, dst) in enumerate(((p1s, p1r), (t1s, t1r)))
        ]

    def l2(step, m):
        places = [(1, far)] if step == OWN else [(0, next_sec), (1, far_of)]
        return [
            move(
                src.at[step, m], dst.at[place, m], l2send.at[step, m, i, place],
                l2recv.at[m, i, place], device,
            )
            for i, (src, dst) in enumerate(((p2s, p2r), (t2s, t2r)))
            for place, device in places
        ]

    def y_forward(m):
        return move(sent.at[m], incf.at[m], ysend.at[m], yrecv.at[m], next_sec)

    def y_back(m):
        return move(dxb.at[m], incb.at[m], wsend.at[m], wrecv.at[m], prev_sec)

    factors = (scaled, hidden, gb, dpre_s)

    def factor_move(which, m, k):
        ref = factors[which].at[x, m]
        return move(ref, ref, fsend.at[which, m, k], frecv.at[which, m, k], x_peers[k])

    def factor_send(which, m):
        for k in range(3):
            factor_move(which, m, k).start()

    def factor_wait(which):
        def wait(m):
            for k in range(3):
                ref = factors[which].at[(x + NX - 1 - k) % NX, m]
                move(ref, ref, fsend.at[which, m, k], frecv.at[which, m, k], x_peers[k]).wait_recv()

        each(wait)

    def enter_begin(step, m, rows, gain, gd, w):
        mean = jnp.sum(rows, 1, keepdims=True) / cols
        centred = rows - mean
        spread = jnp.sum(centred * centred, 1, keepdims=True)
        p1s[step, m] = by_rows((centred * gain).astype(BF16), weights(w))
        put_stat(t1s.at[step, m], mean, spread, gd)
        for copy in l1(step, m):
            copy.start()

    def enter_end(step, m):
        for copy in l1(step, m):
            copy.wait_recv()
        part, mean, spread, gd = join(
            float(cols), p1s[step, m], *get_stat(t1s.at[step, m]),
            p1r[step, m], *get_stat(t1r.at[step, m])
        )
        p2s[step, m] = part.astype(BF16)
        put_stat(t2s.at[step, m], mean, spread, gd)
        if step == OWN:
            p2r[0, m] = part.astype(BF16)
            put_stat(t2r.at[0, m], mean, spread, gd)
        for copy in l2(step, m):
            copy.start()

    def l2_arrival(place, m):
        for i, dst in enumerate((p2r, t2r)):
            move(
                dst.at[place, m], dst.at[place, m], l2send.at[HOP, m, i, place],
                l2recv.at[m, i, place], far,
            ).wait_recv()

    @pl.when(sec == 0)
    def _():
        own_gain_down[...] = gain_times(gain_ref[...], DOWN)

        def enter(m):
            span = to_column(spans[0:1], m * ROWS)
            rows = copies[0, slots[m]].astype(F32) + span * entry[m].astype(F32)
            xs[m] = rows
            enter_begin(OWN, m, rows, gain_ref[...], own_gain_down[...], DOWN)
            enter_end(OWN, m)

        each(enter)

    if_has(NEXT_DOWN, lambda: x_forward(1, NEXT_DOWN))
    x_finish(UP)

    @pl.when(sec > 0)
    def _():
        for p in range(2):
            x_forward(p, PREV_UP)

    @pl.when(sec < last)
    def _():
        x_finish(NEXT_DOWN)
        shard_move(None).wait_recv()
        next_gain_down[...] = gain_times(next_gain[...], NEXT_DOWN)

    def b1(step, m):
        return move(u1s.at[step, m], u1r.at[step, m], b1send.at[step, m], b1recv.at[step, m], mate)

    def b2(step, m):
        places = [(1, far)] if step == OWN else [(0, prev_sec), (1, far_before)]
        return [
            move(
                u2s.at[step, m], u2r.at[place, m], b2send.at[step, m, place],
                b2recv.at[m, place], device,
            )
            for place, device in places
        ]

    def b2_arrival(place, m):
        move(
            u2r.at[place, m], u2r.at[place, m], b2send.at[HOP, m, place],
            b2recv.at[m, place], far,
        ).wait_recv()

    def back_begin(step, m, rows, w):
        u1s[step, m] = by_rows(rows, weights(w))
        b1(step, m).start()

    def back_end(step, m):
        b1(step, m).wait_recv()
        both = (u1s[step, m] + u1r[step, m]).astype(BF16)
        u2s[step, m] = both
        if step == OWN:
            u2r[0, m] = both
        for copy in b2(step, m):
            copy.start()

    def backward(m):
        b2_arrival(1, m)
        grad_act = u2r[0, m].astype(F32) + u2r[1, m].astype(F32)
        pre = pres[m]
        bend = jnp.tanh(CURVE * (pre + 0.044715 * (pre * pre * pre)))
        slope = 0.5 * (1.0 + bend) + 0.5 * pre * (1.0 - bend * bend) * (
            CURVE * (1.0 + 3.0 * 0.044715 * pre * pre)
        )
        dpre = (grad_act * slope).astype(BF16)
        dpre_s[x, m] = dpre
        factor_send(3, m)
        wide = dpre.astype(F32)
        mean_grad = jnp.sum(wide * gsum[...], 1, keepdims=True) / total
        mean_cross = jnp.sum(wide * pre, 1, keepdims=True) / total
        mean, inverse = norm_stat[m, 0], norm_stat[m, 1]
        normed = (xs[m] - mean) * inverse
        dn = times(dpre, weights(DOWN)) * gain_ref[...]
        dx = gs[m] + inverse * (dn - mean_grad - normed * mean_cross)
        gs[m] = dx
        dxb[m] = dx.astype(BF16)

        @pl.when(sec > 0)
        def _():
            y_back(m).start()
            back_begin(HOP, m, dxb[m], PREV_UP)

        peak_src[0:1] += to_lanes(jnp.max(jnp.abs(dx), 1, keepdims=True), m * ROWS)

        @pl.when(sec > 0)
        def _():
            back_end(HOP, m)

    peak_src[...] = jnp.zeros((8, 128), F32)

    @pl.when(sec == last)
    def _():
        def enter(m):
            gs[m] = exit_codes[m].astype(F32) * exit_scale[m]
            gb[x, m] = gs[m].astype(BF16)
            back_begin(OWN, m, gb[x, m], UP)
            factor_send(2, m)
            back_end(OWN, m)

        each(enter)
        x_finish(PREV_UP)

    def forward(m):
        @pl.when(sec > 0)
        def _():
            y_forward(m).wait_recv()
            span = to_column(spans[0:1], m * ROWS)
            xs[m] = copies[0, slots[m]].astype(F32) + span * incf[m].astype(F32)
            l2_arrival(0, m)

        l2_arrival(1, m)
        raw, mean, spread, gd = join(
            float(2 * cols), p2r[0, m].astype(F32), *get_stat(t2r.at[0, m]),
            p2r[1, m].astype(F32), *get_stat(t2r.at[1, m])
        )
        inverse = lax.rsqrt(spread / total + 1e-05)
        pre = raw * inverse
        gsum[...] = gd
        pres[m] = pre
        norm_stat[m, 0] = mean
        norm_stat[m, 1] = inverse
        act = (0.5 * pre * (1.0 + jnp.tanh(CURVE * (pre + 0.044715 * (pre * pre * pre))))).astype(BF16)
        hidden[x, m] = act
        result = xs[m] + times(act, weights(UP))
        span = to_column(spans[1:2], m * ROWS)
        copy_out = copies[1, slots[m]].astype(F32)
        codes = jnp.clip((result - copy_out) / span, -1.0, 1.0).astype(BF16)
        sent[m] = codes

        @pl.when(sec < last)
        def _():
            y_forward(m).start()
            rows = copy_out + span * codes.astype(F32)
            enter_begin(HOP, m, rows, next_gain[...], next_gain_down[...], NEXT_DOWN)

        scaled[x, m] = ((xs[m] - mean) * inverse * gain_ref[...]).astype(BF16)
        factor_send(0, m)
        factor_send(1, m)

        @pl.when(sec < last)
        def _():
            enter_end(HOP, m)

        @pl.when(sec == last)
        def _():
            backward(m)

    each(forward)

    @pl.when(sec < last)
    def _():
        @pl.when(sec > 0)
        def _():
            x_finish(PREV_UP)

        def back(m):
            y_back(m).wait_recv()
            gs[m] = incb[m].astype(F32)
            gb[x, m] = incb[m]
            factor_send(2, m)
            b2_arrival(0, m)
            backward(m)

        each(back)

    quarter = nz // 2
    parity = z % 2

    def unit_pick(side):
        shape = (bot, quarter * unit)
        row = lax.broadcasted_iota(jnp.int32, shape, 0)
        col = lax.broadcasted_iota(jnp.int32, shape, 1)
        source = col + (x * nz + side) * unit
        for k in range(1, quarter):
            source += jnp.where(col >= k * unit, unit, 0)
        return jnp.where(row == source, 1.0, 0.0).astype(BF16)

    def gradient(p, side):
        left, right = (hidden, gb) if p < 2 else (dpre_s, scaled)
        tokens = NX * MICRO * ROWS
        at = slice(p % 2 * half, (p % 2 + 1) * half)
        lhs = times(left[...].reshape(tokens, bot), unit_pick(side)).astype(BF16)
        return by_cols(lhs, right[:, :, :, at].reshape(tokens, half))

    def pair_move(p):
        return move(pair_out.at[p], pair_in.at[p], psend.at[p], precv.at[p], z_mate)

    def gz_move(k):
        slot = (z + 2 * (k + 1)) % nz // 2
        return move(zs.at[slot], rz.at[k], gzsend.at[k], gzrecv.at[k], z_peers[k])

    def piece_rows(p):
        shape = (quarter * 4 * unit, quarter * unit)
        row = lax.broadcasted_iota(jnp.int32, shape, 0)
        col = lax.broadcasted_iota(jnp.int32, shape, 1)
        target = col + p * unit
        for k in range(1, quarter):
            target += jnp.where(col >= k * unit, 3 * unit, 0)
        return jnp.where(row == target, 1.0, 0.0).astype(BF16)

    def gradient_first(pieces):
        for p in pieces:
            pair_out[p] = gradient(p, 1 - parity).astype(BF16)
            pair_move(p).start()
        for p in pieces:
            own[p] = gradient(p, parity)

    def gradient_second():
        rows = 0.0
        for p in range(4):
            pair_move(p).wait_recv()
            both = (own[p] + pair_in[p].astype(F32)).astype(BF16)
            rows += times(piece_rows(p), both)
        zs[...] = rows.astype(BF16).reshape(quarter, 4 * unit, half)
        for k in range(3):
            gz_move(k).start()

    def peak_move(k):
        return move(peak_src, peak_in.at[k], peak_sem.at[0, k], peak_sem.at[1, k], others[k])

    for k in range(3):
        peak_move(k).start()
    factor_wait(0)
    factor_wait(3)
    gradient_first((2, 3))
    factor_wait(1)
    factor_wait(2)
    gradient_first((0, 1))
    gradient_second()

    for k in range(3):
        peak_move(k).wait_recv()
    peak_row = jnp.maximum(
        jnp.maximum(peak_src[0:1], peak_in[0, 0:1]),
        jnp.maximum(peak_in[1, 0:1], peak_in[2, 0:1]),
    )
    peak_row = (peak_row + 1e-05).astype(BF16).astype(F32)

    def codes_back(m):
        returned[m] = (gs[m] / to_column(peak_row, m * ROWS)).astype(BF16)

    each(codes_back)

    result = zs[z // 2].astype(F32)
    for k in range(3):
        gz_move(k).wait_recv()
        result += rz[k].astype(F32)
    own[0] = result
    for p in range(4):
        out = grad_up if p < 2 else grad_down
        out[:, p % 2 * half : (p % 2 + 1) * half] = own[0, p * unit : (p + 1) * unit]

    for k in range(3):
        span_move(k).wait_send()
        peak_move(k).wait_send()

    def drain_micro(m):
        @pl.when(sec == 0)
        def _():
            for copy in l1(OWN, m) + l2(OWN, m):
                copy.wait_send()

        @pl.when(sec == last)
        def _():
            for copy in [b1(OWN, m)] + b2(OWN, m):
                copy.wait_send()

        @pl.when(sec < last)
        def _():
            for copy in l1(HOP, m) + l2(HOP, m) + [y_forward(m)]:
                copy.wait_send()

        @pl.when(sec > 0)
        def _():
            for copy in [b1(HOP, m)] + b2(HOP, m) + [y_back(m)]:
                copy.wait_send()

    each(drain_micro)

    @pl.when(sec > 0)
    def _():
        shard_move(NEXT_DOWN).wait_send()
        shard_move(None).wait_send()

    @pl.when(sec < last)
    def _():
        shard_move(PREV_UP).wait_send()

    for m in ALL:
        def drain_x():
            for p in range(2):
                for kind in range(4):
                    x_move(p, m, kind).wait_send()

        if_has(m, drain_x)

    for p in range(4):
        pair_move(p).wait_send()
    for k in range(3):
        gz_move(k).wait_send()

    def drain_factors(m):
        for which in range(4):
            for k in range(3):
                factor_move(which, m, k).wait_send()

    each(drain_factors)

    def drain_z(slot, carry):
        for m in ALL:
            def drain():
                @pl.when((z < nz - 1) & (slot <= z))
                def _():
                    z_move(0, slot, m).wait_send()

                @pl.when((z > 0) & (slot >= z))
                def _():
                    z_move(1, slot, m).wait_send()

            if_has(m, drain)

        return carry

    lax.fori_loop(0, nz, drain_z, 0)


def solution(mesh):
    nz = mesh.shape["dp"] // NX

    def local(stored, entry, exit_codes, exit_scales, slot_ids, gain, down, up):
        unit, cols = down.shape[1], down.shape[2]
        bot = unit * mesh.shape["dp"]
        tokens = MICRO * ROWS
        pad = lambda w: jnp.pad(w, ((0, PAD - unit), (0, 0)))
        shard = jnp.stack([pad(down[0]), pad(up[0])])
        block = (MICRO, ROWS, cols)
        small = (MICRO, ROWS, bot)
        stat = (2, MICRO, 8, 128)
        dma = pltpu.SemaphoreType.DMA
        vm = pltpu.VMEM
        xrows = bot // NX
        scratch = [
            vm((nz, 4, PAD, cols), BF16),
            vm((4, NX, 2, xrows // 2, cols), BF16),
            vm((8, 128), F32), vm((3, 8, 128), F32), vm((8, 128), F32),
            vm(block, BF16), vm(block, BF16),
            vm(block, F32),
            vm((MICRO, 2, ROWS, 1), F32),
            vm(small, F32),
            vm((1, bot), F32), vm((1, bot), F32), vm((1, bot), F32), vm((1, cols), F32),
            vm((2, *small), F32), vm((2, *small), F32), vm(stat, F32), vm(stat, F32),
            vm((2, *small), BF16), vm((2, *small), BF16), vm(stat, F32), vm(stat, F32),
            vm((2, *small), F32), vm((2, *small), F32),
            vm((2, *small), BF16), vm((2, *small), BF16),
            vm(block, F32), vm(block, BF16),
            vm((8, 128), F32), vm((3, 8, 128), F32),
            vm((NX, *block), BF16), vm((NX, *small), BF16),
            vm((NX, *block), BF16), vm((NX, *small), BF16),
            vm((4, xrows // 2, cols // 2), BF16), vm((4, xrows // 2, cols // 2), BF16),
            vm((4, xrows // 2, cols // 2), F32),
            vm((nz // 2, 4 * unit, cols // 2), BF16),
            vm((3, 4 * unit, cols // 2), BF16),
            dma((2, 3)),
            dma((3,)), dma((3,)),
            dma((2, nz, 4)), dma((nz, 4)),
            dma((2, 4, 4)), dma((2, 4, 4)),
            dma((2, MICRO, 2)), dma((2, MICRO, 2)), dma((2, MICRO, 2, 2)), dma((MICRO, 2, 2)),
            dma((2, MICRO)), dma((2, MICRO)), dma((2, MICRO, 2)), dma((MICRO, 2)),
            dma((MICRO,)), dma((MICRO,)), dma((MICRO,)), dma((MICRO,)),
            dma((2, 3)),
            dma((4, MICRO, 3)), dma((4, MICRO, 3)),
            dma((4,)), dma((4,)),
            dma((3,)), dma((3,)),
        ]
        in_vmem = pl.BlockSpec(memory_space=pltpu.VMEM)
        sent, returned, grad_down, grad_up = pl.pallas_call(
            lambda *refs: relay_kernel(nz, *refs),
            out_shape=(
                jax.ShapeDtypeStruct(block, BF16),
                jax.ShapeDtypeStruct(block, BF16),
                jax.ShapeDtypeStruct((unit, cols), F32),
                jax.ShapeDtypeStruct((unit, cols), F32),
            ),
            in_specs=[in_vmem] * 4 + [pl.BlockSpec(memory_space=pltpu.SMEM)] + [in_vmem] * 2,
            out_specs=(in_vmem,) * 4,
            scratch_shapes=scratch,
            compiler_params=pltpu.CompilerParams(
                collective_id=0, has_side_effects=True, vmem_limit_bytes=48 * 2**20
            ),
        )(
            stored[0].reshape(2, MICRO, ROWS, cols),
            entry.reshape(block),
            exit_codes.reshape(block),
            exit_scales.reshape(MICRO, ROWS, 1),
            slot_ids[0],
            gain,
            shard,
        )
        return (
            sent.reshape(1, tokens, cols),
            returned.reshape(1, tokens, cols),
            grad_down[None],
            grad_up[None],
        )

    in_specs = (
        P("section", None, "dp", "tensor"),
        P("dp", "tensor"),
        P("dp", "tensor"),
        P("dp"),
        P("dp", None),
        P("section", "tensor"),
        P("section", "dp", "tensor"),
        P("section", "dp", "tensor"),
    )
    out_specs = (P("section", "dp", "tensor"),) * 4
    return jax.shard_map(local, mesh=mesh, in_specs=in_specs, out_specs=out_specs, check_vma=False)
```

time: 236 us -> 220 us (0.932); the launches traced: 236 us -> 216 us
  Pallas kernels: 226 us -> 206 us
    pallas_call x1, Pallas kernels: 226 us -> 206 us  [local(): pl.pallas_call(lambda *refs: relay_kernel(nz, *refs), out_shape=(jax.Shap...]
where the time goes in v3:
time: 220 us; the launch traced here: 216 us
  Pallas kernels  206 us (94%)
  local copies, waits for them, and re-layouts  9.69 us (4%)
    pallas_call x1, Pallas kernels, local(): pl.pallas_call(lambda *refs: relay_kernel(nz, *refs), out_shape=(jax.Shap...  206 us
    unnamed x14, local copies, waits for them, and re-layouts  7.89 us

profile of v3, /device:TPU:6, one launch (start us, length us, event | category | flops | bytes accessed | tf_op | source)
XLA Modules:
  0.0 215.9 jit_solution(17428406148700600098)
XLA Ops:
  0.6 0.9 reshape.28.refs_3_
  1.5 0.9 pad_bitcast_fusion
  2.5 0.0 copy-start
  2.5 1.3 copy-done
  3.7 0.0 copy-start.1
  3.7 1.1 copy-done.1
  4.8 0.0 copy-start.2
  4.8 1.1 copy-done.2
  5.9 0.0 copy-start.3
  5.9 0.7 copy-done.3
  6.6 0.0 copy-start.4
  6.6 0.7 copy-done.4
  7.2 205.5 %shard_map.111 = (bf16[4,32,2304]{2,1,0:T(8,128)(2,1)S(1)}, bf16[4,32,2304]{2,1,0:T(8,128)(2,1)S(1)}, f32[12,2304]{1,0:T(8,128)S(1)}, f32[12,2304]{1,0:T(8,128)S(1)}) custom-call(bf16[2,4,32,2304]{3,2,1,0:T(8,128)(2,1)S(1)} %bitcast.14, bf16[4,32,2304]{2,1,0:T(8,128)(2,1)S(1)} %bitcast.17, bf16[4,32,2304]{2,1,0:T(8,128)(2,1)S(1)} %bitcast.18, ...), custom_call_target="tpu_custom_call" | custom-call | tf_op jit(solution)/shard_map/pallas_call | solution.py:763
  212.8 0.8 copy.13
  213.5 0.8 copy.14
  214.3 0.8 copy.17
  215.1 0.8 copy.18
  (1 shorter events, 0.0 us)
Async XLA Ops:
  2.5 1.3 copy-start
  3.7 1.1 copy-start.1
  4.8 1.1 copy-start.2
  5.9 0.7 copy-start.3
  6.6 0.7 copy-start.4

commit v4 on v3

--- a/solution.py
+++ b/solution.py
@@ -45,14 +45,18 @@
     return jnp.sum(jnp.where(lane_mask(shift), lanes, 0.0), 1, keepdims=True)
 
 
-def spread_matrix(shards, unit):
+def shard_rows(shards, unit, part):
     shape = (shards * unit, shards * PAD)
     row = lax.broadcasted_iota(jnp.int32, shape, 0)
     col = lax.broadcasted_iota(jnp.int32, shape, 1)
-    shard = jnp.zeros(shape, jnp.int32)
-    for k in range(1, shards):
-        shard += jnp.where(row >= k * unit, 1, 0)
-    return jnp.where(col == shard * PAD + row - shard * unit, 1.0, 0.0)
+    hit = row < 0
+    for k in range(shards):
+        for i in range(unit if part is None else unit // 3):
+            if part is None:
+                hit |= (row == k * unit + i) & (col == k * PAD + i)
+            else:
+                hit |= (row == k * unit + 3 * i + part) & (col == k * PAD + unit + i)
+    return jnp.where(hit, 1.0, 0.0).astype(BF16)
 
 
 def relay_kernel(
@@ -64,7 +68,7 @@
     gs, dxb, peak_src, peak_in, scaled, hidden, gb, dpre_s, pair_out, pair_in, own, zs, rz,
     span_sem, ssend, srecv, zsend, zrecv, xsend, xrecv, l1send, l1recv, l2send, l2recv,
     b1send, b1recv, b2send, b2recv, ysend, yrecv, wsend, wrecv, peak_sem,
-    fsend, frecv, psend, precv, gzsend, gzrecv,
+    fsend, frecv, rsend, rrecv, psend, precv, gzsend, gzrecv,
 ):
     sec = lax.axis_index("section")
     last = lax.axis_size("section") - 1
@@ -76,6 +80,7 @@
     unit = grad_down.shape[0]
     cols = gain_ref.shape[1]
     half = cols // 2
+    pack = shard.shape[2]
     bot = pres.shape[2]
     total = cols * 4
     xr, xl, xo = (x + 1) % NX, (x + NX - 1) % NX, (x + 2) % NX
@@ -194,9 +199,15 @@
         move(ref, ref, xsend.at[p, m, kind], xrecv.at[p, m, kind], to_right).wait_recv()
 
     def x_own(p, m):
-        block = zbuf[pl.ds(group[p] * half_z, half_z), m].reshape(half_z * PAD, cols)
-        pick = spread_matrix(half_z, unit).astype(BF16)
-        wv[m, x, group[p]] = times(pick, block).astype(BF16)
+        g = group[p]
+        block = zbuf[pl.ds(g * half_z, half_z), m].reshape(half_z * PAD, pack)
+        wv[m, x, g, :, 0:pack] = times(shard_rows(half_z, unit, None), block).astype(BF16)
+        tail = 0.0
+        for j in range(3):
+            tail += times(
+                shard_rows(half_z, unit, j), block[:, j * (cols - pack) : (j + 1) * (cols - pack)]
+            )
+        wv[m, x, g, :, pack:cols] = tail.astype(BF16)
         x_move(p, m, 0).start()
         x_move(p, m, 1).start()
 
@@ -261,19 +272,20 @@
     z_steps(half_z + 2, half_z + 3)
     x_forward(0, UP)
     z_steps(half_z + 3, nz)
-    for m in (DOWN, UP, NEXT_DOWN):
-        if_has(m, lambda: x_own(1, m))
+    x_own(1, DOWN)
+    x_own(1, UP)
     if_has(NEXT_DOWN, lambda: x_forward(0, NEXT_DOWN))
-    for p in range(2):
-        if_has(PREV_UP, lambda: x_own(p, PREV_UP))
     for k in range(3):
         span_move(k).wait_recv()
     spans[...] = 2.0 * jnp.sqrt(
         (span_src[...] + span_in[0] + span_in[1] + span_in[2]) / total + 1e-05
     )
     x_forward(1, DOWN)
+    if_has(NEXT_DOWN, lambda: x_own(1, NEXT_DOWN))
     x_forward(1, UP)
     x_finish(DOWN)
+    for p in range(2):
+        if_has(PREV_UP, lambda: x_own(p, PREV_UP))
 
     def weights(m):
         return wv[m].reshape(bot, cols)
@@ -333,7 +345,7 @@
     def y_back(m):
         return move(dxb.at[m], incb.at[m], wsend.at[m], wrecv.at[m], prev_sec)
 
-    factors = (scaled, hidden, gb, dpre_s)
+    factors = (hidden, dpre_s)
 
     def factor_move(which, m, k):
         ref = factors[which].at[x, m]
@@ -350,6 +362,49 @@
                 move(ref, ref, fsend.at[which, m, k], frecv.at[which, m, k], x_peers[k]).wait_recv()
 
         each(wait)
+
+    ring_rows = (scaled, gb)
+
+    def ring_move(which, m, kind):
+        block, device, part = {
+            0: (x, to_right, slice(None)),
+            1: (x, to_left, slice(None)),
+            2: (xl, to_right, slice(0, half)),
+            3: (xr, to_left, slice(half, cols)),
+        }[kind]
+        rows = ring_rows[which]
+        ref = rows.at[block, m] if kind < 2 else rows.at[block, m, :, part]
+        return move(ref, ref, rsend.at[which, m, kind], rrecv.at[which, m, kind], device)
+
+    def ring_arrival(which, m, kind):
+        rows = ring_rows[which]
+        ref = {
+            0: lambda: rows.at[xl, m],
+            1: lambda: rows.at[xr, m],
+            2: lambda: rows.at[xo, m, :, slice(0, half)],
+            3: lambda: rows.at[xo, m, :, slice(half, cols)],
+        }[kind]()
+        move(ref, ref, rsend.at[which, m, kind], rrecv.at[which, m, kind], to_right).wait_recv()
+
+    def ring_send(which, m):
+        ring_move(which, m, 0).start()
+        ring_move(which, m, 1).start()
+
+    def ring_forward(which):
+        def step(m):
+            ring_arrival(which, m, 0)
+            ring_move(which, m, 2).start()
+            ring_arrival(which, m, 1)
+            ring_move(which, m, 3).start()
+
+        each(step)
+
+    def ring_end(which):
+        def step(m):
+            ring_arrival(which, m, 2)
+            ring_arrival(which, m, 3)
+
+        each(step)
 
     def enter_begin(step, m, rows, gain, gd, w):
         mean = jnp.sum(rows, 1, keepdims=True) / cols
@@ -451,7 +506,7 @@
         )
         dpre = (grad_act * slope).astype(BF16)
         dpre_s[x, m] = dpre
-        factor_send(3, m)
+        factor_send(1, m)
         wide = dpre.astype(F32)
         mean_grad = jnp.sum(wide * gsum[...], 1, keepdims=True) / total
         mean_cross = jnp.sum(wide * pre, 1, keepdims=True) / total
@@ -481,7 +536,7 @@
             gs[m] = exit_codes[m].astype(F32) * exit_scale[m]
             gb[x, m] = gs[m].astype(BF16)
             back_begin(OWN, m, gb[x, m], UP)
-            factor_send(2, m)
+            ring_send(1, m)
             back_end(OWN, m)
 
         each(enter)
@@ -521,8 +576,8 @@
             enter_begin(HOP, m, rows, next_gain[...], next_gain_down[...], NEXT_DOWN)
 
         scaled[x, m] = ((xs[m] - mean) * inverse * gain_ref[...]).astype(BF16)
+        ring_send(0, m)
         factor_send(0, m)
-        factor_send(1, m)
 
         @pl.when(sec < last)
         def _():
@@ -533,6 +588,7 @@
             backward(m)
 
     each(forward)
+    ring_forward(0)
 
     @pl.when(sec < last)
     def _():
@@ -544,11 +600,13 @@
             y_back(m).wait_recv()
             gs[m] = incb[m].astype(F32)
             gb[x, m] = incb[m]
-            factor_send(2, m)
+            ring_send(1, m)
             b2_arrival(0, m)
             backward(m)
 
         each(back)
+
+    ring_forward(1)
 
     quarter = nz // 2
     parity = z % 2
@@ -607,11 +665,11 @@
 
     for k in range(3):
         peak_move(k).start()
+    ring_end(0)
+    factor_wait(1)
+    gradient_first((2, 3))
     factor_wait(0)
-    factor_wait(3)
-    gradient_first((2, 3))
-    factor_wait(1)
-    factor_wait(2)
+    ring_end(1)
     gradient_first((0, 1))
     gradient_second()
 
@@ -687,9 +745,12 @@
         gz_move(k).wait_send()
 
     def drain_factors(m):
-        for which in range(4):
+        for which in range(2):
             for k in range(3):
                 factor_move(which, m, k).wait_send()
+        for which in range(2):
+            for kind in range(4):
+                ring_move(which, m, kind).wait_send()
 
     each(drain_factors)
 
@@ -718,8 +779,14 @@
         unit, cols = down.shape[1], down.shape[2]
         bot = unit * mesh.shape["dp"]
         tokens = MICRO * ROWS
-        pad = lambda w: jnp.pad(w, ((0, PAD - unit), (0, 0)))
-        shard = jnp.stack([pad(down[0]), pad(up[0])])
+        pack = cols * unit // PAD // 128 * 128 + 128
+
+        def packed(w):
+            tail = w[:, pack:].reshape(PAD - unit, unit // (PAD - unit) * (cols - pack))
+            tail = jnp.pad(tail, ((0, 0), (0, pack - tail.shape[1])))
+            return jnp.concatenate([w[:, :pack], tail])
+
+        shard = jnp.stack([packed(down[0]), packed(up[0])])
         block = (MICRO, ROWS, cols)
         small = (MICRO, ROWS, bot)
         stat = (2, MICRO, 8, 128)
@@ -727,7 +794,7 @@
         vm = pltpu.VMEM
         xrows = bot // NX
         scratch = [
-            vm((nz, 4, PAD, cols), BF16),
+            vm((nz, 4, PAD, pack), BF16),
             vm((4, NX, 2, xrows // 2, cols), BF16),
             vm((8, 128), F32), vm((3, 8, 128), F32), vm((8, 128), F32),
             vm(block, BF16), vm(block, BF16),
@@ -755,7 +822,8 @@
             dma((2, MICRO)), dma((2, MICRO)), dma((2, MICRO, 2)), dma((MICRO, 2)),
             dma((MICRO,)), dma((MICRO,)), dma((MICRO,)), dma((MICRO,)),
             dma((2, 3)),
-            dma((4, MICRO, 3)), dma((4, MICRO, 3)),
+            dma((2, MICRO, 3)), dma((2, MICRO, 3)),
+            dma((2, MICRO, 4)), dma((2, MICRO, 4)),
             dma((4,)), dma((4,)),
             dma((3,)), dma((3,)),
         ]

time: 220 us -> 210 us (0.955)
  the two profiles are of different devices: /device:TPU:6 before, /device:TPU:65 now
where the time goes in v4:
time: 210 us
  Pallas kernels  198 us (94%)
  local copies, waits for them, and re-layouts  10.9 us (5%)
    pallas_call x1, Pallas kernels, local(): pl.pallas_call(lambda *refs: relay_kernel(nz, *refs), out_shape=(jax.Shap...  198 us
    unnamed x14, local copies, waits for them, and re-layouts  6.83 us

profile of v4, /device:TPU:65, one launch (start us, length us, event | category | flops | bytes accessed | tf_op | source)
XLA Modules:
  0.0 209.9 jit_solution(12158840154437206414)
XLA Ops:
  0.6 0.0 copy-start.1
  0.6 0.8 slice.17
  1.4 0.7 slice.19
  2.2 0.8 slice.16
  3.0 0.8 slice.18
  3.9 0.9 reshape.36.refs_3_
  4.8 0.0 copy-done.1
  4.8 0.0 copy-start
  4.8 1.3 copy-done
  6.0 0.0 copy-start.2
  6.0 1.1 copy-done.2
  7.1 0.0 copy-start.3
  7.1 0.7 copy-done.3
  7.8 0.0 copy-start.4
  7.8 0.7 copy-done.4
  8.5 198.3 %shard_map.111 = (bf16[4,32,2304]{2,1,0:T(8,128)(2,1)S(1)}, bf16[4,32,2304]{2,1,0:T(8,128)(2,1)S(1)}, f32[12,2304]{1,0:T(8,128)S(1)}, f32[12,2304]{1,0:T(8,128)S(1)}) custom-call(bf16[2,4,32,2304]{3,2,1,0:T(8,128)(2,1)S(1)} %bitcast.14, bf16[4,32,2304]{2,1,0:T(8,128)(2,1)S(1)} %bitcast.15, bf16[4,32,2304]{2,1,0:T(8,128)(2,1)S(1)} %bitcast.16, ...), custom_call_target="tpu_custom_call" | custom-call | tf_op jit(solution)/shard_map/pallas_call | solution.py:831
  206.8 0.8 copy.13
  207.5 0.8 copy.14
  208.3 0.8 copy.17
  209.1 0.8 copy.18
  (4 shorter events, 0.1 us)
Async XLA Ops:
  0.6 4.1 %copy-start.1 = (bf16[128,2304]{1,0:T(8,128)(2,1)S(1)}, bf16[128,2304]{1,0:T(8,128)(2,1)}, u32[]{:S(2)}) copy-start(bf16[128,2304]{1,0:T(8,128)(2,1)} %param.9) | copy-start | bytes 1769476
  4.8 1.3 copy-start
  6.0 1.1 copy-start.2
  7.1 0.7 copy-start.3
  7.8 0.7 copy-start.4

commit v5 on v4

--- a/solution.py
+++ b/solution.py
@@ -16,6 +16,7 @@
 PAD = 16
 DOWN, UP, NEXT_DOWN, PREV_UP = ALL = (0, 1, 2, 3)
 OWN, HOP = 0, 1
+LAG = 2
 CURVE = math.sqrt(2.0 / math.pi)
 
 
@@ -147,10 +148,12 @@
         def _():
             z_move(1, z, m).start()
 
-    def z_step(k):
+    def z_step(tick):
         for m in ALL:
+            k = tick if m in (DOWN, UP) else tick - LAG
+
             def pass_on():
-                @pl.when(z - k >= 0)
+                @pl.when((k >= 1) & (z - k >= 0))
                 def _():
                     z_move(0, z - k, m).wait_recv()
 
@@ -158,7 +161,7 @@
                     def _():
                         z_move(0, z - k, m).start()
 
-                @pl.when(z + k < nz)
+                @pl.when((k >= 1) & (z + k < nz))
                 def _():
                     z_move(1, z + k, m).wait_recv()
 
@@ -265,16 +268,18 @@
         z_begin(PREV_UP)
 
     z_steps(1, half_z)
-    for m in (DOWN, UP, NEXT_DOWN):
-        if_has(m, lambda: x_own(0, m))
-    z_steps(half_z, half_z + 2)
+    x_own(0, DOWN)
+    x_own(0, UP)
+    z_steps(half_z, half_z + LAG)
+    if_has(NEXT_DOWN, lambda: x_own(0, NEXT_DOWN))
     x_forward(0, DOWN)
-    z_steps(half_z + 2, half_z + 3)
+    z_steps(half_z + LAG, half_z + LAG + 1)
     x_forward(0, UP)
-    z_steps(half_z + 3, nz)
+    z_steps(half_z + LAG + 1, nz)
     x_own(1, DOWN)
     x_own(1, UP)
     if_has(NEXT_DOWN, lambda: x_forward(0, NEXT_DOWN))
+    z_steps(nz, nz + LAG)
     for k in range(3):
         span_move(k).wait_recv()
     spans[...] = 2.0 * jnp.sqrt(
@@ -647,12 +652,14 @@
         for p in pieces:
             pair_out[p] = gradient(p, 1 - parity).astype(BF16)
             pair_move(p).start()
-        for p in pieces:
+
+    def gradient_own():
+        for p in range(4):
             own[p] = gradient(p, parity)
 
     def gradient_second():
         rows = 0.0
-        for p in range(4):
+        for p in (2, 3, 0, 1):
             pair_move(p).wait_recv()
             both = (own[p] + pair_in[p].astype(F32)).astype(BF16)
             rows += times(piece_rows(p), both)
@@ -671,6 +678,7 @@
     factor_wait(0)
     ring_end(1)
     gradient_first((0, 1))
+    gradient_own()
     gradient_second()
 
     for k in range(3):

time: 210 us -> 207 us (0.986)
  the two profiles are of different devices: /device:TPU:65 before, /device:TPU:6 now
where the time goes in v5:
time: 207 us; the launch traced here: 204 us
  Pallas kernels  192 us (93%)
  local copies, waits for them, and re-layouts  10.9 us (5%)
    pallas_call x1, Pallas kernels, local(): pl.pallas_call(lambda *refs: relay_kernel(nz, *refs), out_shape=(jax.Shap...  192 us
    unnamed x14, local copies, waits for them, and re-layouts  6.83 us

profile of v5, /device:TPU:6, one launch (start us, length us, event | category | flops | bytes accessed | tf_op | source)
XLA Modules:
  0.0 203.7 jit_solution(13945410189216537653)
XLA Ops:
  0.6 0.0 copy-start.1
  0.6 0.8 slice.17
  1.4 0.7 slice.19
  2.2 0.8 slice.16
  3.0 0.8 slice.18
  3.9 0.9 reshape.36.refs_3_
  4.8 0.0 copy-done.1
  4.8 0.0 copy-start
  4.8 1.3 copy-done
  6.0 0.0 copy-start.2
  6.0 1.1 copy-done.2
  7.1 0.0 copy-start.3
  7.1 0.7 copy-done.3
  7.8 0.0 copy-start.4
  7.8 0.7 copy-done.4
  8.5 192.0 %shard_map.111 = (bf16[4,32,2304]{2,1,0:T(8,128)(2,1)S(1)}, bf16[4,32,2304]{2,1,0:T(8,128)(2,1)S(1)}, f32[12,2304]{1,0:T(8,128)S(1)}, f32[12,2304]{1,0:T(8,128)S(1)}) custom-call(bf16[2,4,32,2304]{3,2,1,0:T(8,128)(2,1)S(1)} %bitcast.14, bf16[4,32,2304]{2,1,0:T(8,128)(2,1)S(1)} %bitcast.15, bf16[4,32,2304]{2,1,0:T(8,128)(2,1)S(1)} %bitcast.16, ...), custom_call_target="tpu_custom_call" | custom-call | tf_op jit(solution)/shard_map/pallas_call | solution.py:839
  200.5 0.8 copy.13
  201.3 0.8 copy.14
  202.0 0.8 copy.17
  202.8 0.8 copy.18
  (4 shorter events, 0.1 us)
Async XLA Ops:
  0.6 4.1 %copy-start.1 = (bf16[128,2304]{1,0:T(8,128)(2,1)S(1)}, bf16[128,2304]{1,0:T(8,128)(2,1)}, u32[]{:S(2)}) copy-start(bf16[128,2304]{1,0:T(8,128)(2,1)} %param.9) | copy-start | bytes 1769476
  4.8 1.3 copy-start
  6.0 1.1 copy-start.2
  7.1 0.7 copy-start.3
  7.8 0.7 copy-start.4
